TPU v7x, 32 devices: a whole 2x2x4 slice. The times are simulated.
32 devices in a mesh: section: 2 (over core), row: 8 (over z, x), col: 2 (over y).
Axes of the slice: x: 2, y: 2, z: 4, core: 2. Of those that a mesh axis runs over, the one named last changes fastest.
Arguments:
- prior_root: float32 [512, 32, 2, 256], P(None, None, 'col'), may hold values from -0.08 to 4, as said below
- observations: float32 [2, 1024, 32, 2, 256], P('section', 'row', None, 'col'), may hold values from -0.5 to 0.5
- live_rows: int32 [2, 8], P('section', 'row'), may hold values from 1 to 128, 640 in all within a row
Outputs:
- r_slab: float32 [2, 512, 32, 2, 256], P('section', 'row', None, 'col')
Inputs may be any that keep to these rules, and one draw needn't show every extreme that they name: `prior_root`: zero where the global column is below the row, positive on the diagonal. `live_rows`: within one arc group the counts sum to 640; the largest count of each arc group is 128.
All inputs are finite; a program needn't handle non-finite values.
Results may differ from a plain program's by a relative error of at most 0.0001.
Values sent between devices are 32-bit elements; how exact they have to be, the bound alone decides.
No kernel may reach another device: no remote copies, remote signals or barrier semaphores. Data moves between devices by JAX's collectives and lax.ppermute only.
A program may use at most 192 MiB of HBM per device.

v0:
```python
import functools

import jax
import jax.numpy as jnp
from jax import lax
from jax.experimental import pallas as pl
from jax.experimental.pallas import tpu as pltpu
from jax.sharding import PartitionSpec as P

LANES = 128
TALL = 16
GROUP = 8
SPOTS = 6
VMEM_BYTES = 56 * 2**20


def dot(left, right, contract_left, contract_right):
    return lax.dot_general(
        left,
        right,
        (((contract_left,), (contract_right,)), ((), ())),
        precision=lax.Precision.HIGHEST,
        preferred_element_type=jnp.float32,
    )


def thirds(value):
    high = value.astype(jnp.bfloat16)
    rest = value - high.astype(jnp.float32)
    middle = rest.astype(jnp.bfloat16)
    return high, middle, (rest - middle.astype(jnp.float32)).astype(jnp.bfloat16)


def short_dot(left, right, contract_left, contract_right):
    a, b = thirds(left), thirds(right)
    left = jnp.concatenate([a[0], a[0], a[1], a[1], a[0], a[2]], axis=contract_left)
    right = jnp.concatenate([b[0], b[1], b[0], b[1], b[2], b[0]], axis=contract_right)
    return lax.dot_general(
        left,
        right,
        (((contract_left,), (contract_right,)), ((), ())),
        preferred_element_type=jnp.float32,
    )


def spread(row, shape):
    return jnp.broadcast_to(row, shape)


def factor_block(work_ref):
    size = work_ref.shape[0]
    tile = (8, LANES)
    row_ids = lax.broadcasted_iota(jnp.int32, tile, 0)
    for first in range(0, size, TALL):
        middle, end = first + 8, first + TALL
        top = [work_ref[first:middle, t * LANES : (t + 1) * LANES] for t in range(2)]
        low = [work_ref[middle:end, t * LANES : (t + 1) * LANES] for t in range(2)]
        top_col = [spread(top[0][:, first + k : first + k + 1], tile) for k in range(TALL)]
        low_col = [spread(low[0][:, first + k : first + k + 1], tile) for k in range(TALL)]
        top_pivot = jnp.ones(tile, jnp.float32)
        low_pivot = jnp.ones(tile, jnp.float32)
        for step in range(TALL):
            if step < 8:
                pivot = spread(top_col[step][step : step + 1], tile)
                inverse = 1.0 / pivot
                top_by = jnp.where(row_ids > step, top_col[step] * inverse, 0.0)
                low_by = low_col[step] * inverse
                top_pivot = jnp.where(row_ids == step, pivot, top_pivot)
                for k in range(step + 1, TALL):
                    lead = spread(top_col[k][step : step + 1], tile)
                    top_col[k] = top_col[k] - top_by * lead
                    low_col[k] = low_col[k] - low_by * lead
                for t in range(2):
                    lead = spread(top[t][step : step + 1], tile)
                    top[t] = top[t] - top_by * lead
                    low[t] = low[t] - low_by * lead
            else:
                at = step - 8
                pivot = spread(low_col[step][at : at + 1], tile)
                low_by = jnp.where(row_ids > at, low_col[step] * (1.0 / pivot), 0.0)
                low_pivot = jnp.where(row_ids == at, pivot, low_pivot)
                for k in range(step + 1, TALL):
                    low_col[k] = low_col[k] - low_by * spread(low_col[k][at : at + 1], tile)
                for t in range(2):
                    low[t] = low[t] - low_by * spread(low[t][at : at + 1], tile)
        top_scale, low_scale = lax.rsqrt(top_pivot), lax.rsqrt(low_pivot)
        for t in range(2):
            work_ref[first:middle, t * LANES : (t + 1) * LANES] = top[t] * top_scale
            work_ref[middle:end, t * LANES : (t + 1) * LANES] = low[t] * low_scale
        if end < size:
            done = work_ref[first:end, :]
            change = short_dot(done[:, :LANES], done, 0, 0)
            work_ref[end:, :] = work_ref[end:, :] - change[end:, :]


def factor_kernel(own_ref, other_ref, inverse_ref, info_ref, work_ref):
    size = own_ref.shape[0]
    ids = [lax.broadcasted_iota(jnp.int32, (LANES, LANES), axis) for axis in range(2)]
    eye = (ids[0] == ids[1]).astype(jnp.float32)
    info_ref[...] = own_ref[...] + other_ref[...]
    inverse_ref[...] = jnp.zeros_like(inverse_ref)
    for start in range(0, size, LANES):
        end = start + LANES
        work_ref[:, :LANES] = info_ref[start:end, start:end]
        work_ref[:, LANES:] = eye
        factor_block(work_ref)
        block = work_ref[:, LANES:]
        if start:
            inverse_ref[start:end, :start] = short_dot(block, inverse_ref[start:end, :start], 1, 0)
        inverse_ref[start:end, start:end] = block
        if end < size:
            upper = short_dot(block, info_ref[start:end, end:], 1, 0)
            info_ref[end:, end:] = info_ref[end:, end:] - short_dot(upper, upper, 0, 0)
            inverse_ref[end:, :end] = inverse_ref[end:, :end] - short_dot(
                upper, inverse_ref[start:end, :end], 0, 0
            )


def vmem_spec():
    return pl.BlockSpec(memory_space=pltpu.VMEM)


def params():
    return pltpu.CompilerParams(vmem_limit_bytes=VMEM_BYTES)


def shape_of(*shape):
    return jax.ShapeDtypeStruct(shape, jnp.float32)


def factor(own, other):
    size = own.shape[0]
    return pl.pallas_call(
        factor_kernel,
        out_shape=shape_of(size, size),
        in_specs=[vmem_spec()] * 2,
        out_specs=vmem_spec(),
        scratch_shapes=[
            pltpu.VMEM((size, size), jnp.float32),
            pltpu.VMEM((LANES, 2 * LANES), jnp.float32),
        ],
        compiler_params=params(),
        name="factor",
    )(own, other)


def panel_kernel(count, spot_ref, near_ref, *refs):
    near_prior, far_prior, rows_ref, prior_ref, gram_ref = refs[-5:]
    parts = refs[:-5]
    width = near_prior.shape[1]
    col, section = spot_ref[0], spot_ref[1]
    near_at = pl.ds(pl.multiple_of(col * width, width), width)
    far_at = pl.ds(pl.multiple_of((1 - col) * width, width), width)
    slots = near_ref.shape[0] * 2 // count
    near_next, far_here, far_next = parts
    pair = spot_ref[2] // 2
    for i in range(count // 2):
        here, beside = (pl.ds(((pair ^ i) + side) * slots, slots) for side in (0, count // 2))
        piece = slice(i * slots, (i + 1) * slots)
        rows_ref[here, near_at] = near_ref[piece]
        rows_ref[beside, near_at] = near_next[piece]
        rows_ref[here, far_at] = far_here[piece]
        rows_ref[beside, far_at] = far_next[piece]
    keep = (section == 0).astype(jnp.float32)
    prior_ref[:, near_at] = near_prior[...] * keep
    prior_ref[:, far_at] = far_prior[...] * keep
    left = rows_ref[:, :width]
    right = rows_ref[:, width:]
    prior = prior_ref[:width, :]
    gram_ref[:width, :] = dot(left, rows_ref[...], 0, 0) + dot(prior[:, :width], prior, 0, 0)
    corner = prior_ref[:, width:]
    gram_ref[width:, width:] = dot(right, right, 0, 0) + dot(corner, corner, 0, 0)
    gram_ref[width:, :width] = jnp.zeros((width, width), jnp.float32)


def panel_gram(count, spot, parts, near_prior, far_prior):
    slots = parts[0].shape[0] * 2 // count
    total, width = near_prior.shape
    return pl.pallas_call(
        functools.partial(panel_kernel, count),
        out_shape=(
            shape_of(count * slots, 2 * width),
            shape_of(total, 2 * width),
            shape_of(total, total),
        ),
        in_specs=[pl.BlockSpec(memory_space=pltpu.SMEM)] + [vmem_spec()] * 6,
        out_specs=(vmem_spec(),) * 3,
        compiler_params=params(),
        name="panel_gram",
    )(spot, *parts, near_prior, far_prior)


def gather_blocks(ref, first, rows, stride, blocks, work, at):
    for b in range(blocks):
        work[at : at + rows, b * LANES : (b + 1) * LANES] = ref[pl.ds(first + b, rows, stride=stride), :]


def pack_kernel(first, each, joined, spot_ref, *refs):
    *sources, out_ref = refs
    outs = [out_ref] if len(out_ref.shape) == 2 else [out_ref.at[i] for i in range(2)]
    if joined:
        outs.pop(0)[...] = sources.pop(0)[...]
    for source, out in zip(sources, outs):
        slots, chunk, _ = source.shape
        flat = source.reshape(slots * chunk, LANES)
        for b in range(each):
            out[pl.ds(b, slots, stride=each), :] = flat[pl.ds(first + b, slots, stride=chunk), :]


def pack(spot, observed, part, each, sides, swapped_blocks=None):
    slots, rows, chunk, _ = observed.shape
    size = slots * each

    def source(side):
        at = lambda i, spot: (0, 2 * i + (spot[2] + side) % 2, 0, 0)
        return pl.BlockSpec((slots, None, chunk, LANES), at)

    specs, arrays = [source(side) for side in sides], [observed] * len(sides)
    if swapped_blocks is not None:
        specs = [pl.BlockSpec((None, size, LANES), lambda i, spot: (i, 0, 0))] + specs
        arrays = [swapped_blocks] + arrays
    if len(specs) == 1:
        out, out_spec = (rows // 2, size), pl.BlockSpec((None, size, LANES), lambda i, spot: (i, 0, 0))
    else:
        out = (rows // 2, 2, size)
        out_spec = pl.BlockSpec((None, 2, size, LANES), lambda i, spot: (i, 0, 0, 0))
    return pl.pallas_call(
        functools.partial(pack_kernel, part * each, each, swapped_blocks is not None),
        out_shape=shape_of(*out, LANES),
        grid_spec=pltpu.PrefetchScalarGridSpec(
            num_scalar_prefetch=1, grid=(rows // 2,), in_specs=specs, out_specs=out_spec
        ),
        compiler_params=params(),
        name="pack",
    )(spot, *arrays)


def plain_pack(spot, observed):
    slots, rows, chunk, _ = observed.shape
    pairs = observed.reshape(slots, rows // 2, 2, chunk, LANES).transpose(1, 2, 0, 3, 4)
    sides = [lax.dynamic_index_in_dim(pairs, (spot[2] + side) % 2, 1, keepdims=False) for side in (1, 0)]
    return jnp.stack(sides, axis=1).reshape(rows // 2, 2, slots * chunk, LANES)


def info_kernel(each, spot_ref, rows_ref, panel_ref, prior_ref, far_ref, near_ref, out_ref, work):
    total, group = prior_ref.shape[0], prior_ref.shape[1]
    count, pairs = rows_ref.shape[0], far_ref.shape[0]
    slots = count // 2 // pairs
    flat = prior_ref.reshape(total * group, LANES)
    gather_blocks(flat, spot_ref[5], total, group, each, work, 0)
    part = dot(panel_ref[...], work[:total, :], 0, 0)
    for i in range(pairs):
        gather_blocks(near_ref.at[i], 0, slots, each, each, work, i * slots)
        gather_blocks(far_ref.at[i], 0, slots, each, each, work, count // 2 + i * slots)
    out_ref[...] = part + dot(rows_ref[...], work[:count, :], 0, 0)


def info_part(each, spot, rows, panel, prior, far, near):
    total, _, group, _ = prior.shape
    full = lambda array: pl.BlockSpec(array.shape, lambda i, spot: (0,) * array.ndim)
    half = lambda array, at: pl.BlockSpec(
        (array.shape[0], None) + array.shape[2:], lambda i, spot: (0, at, 0, 0)
    )
    return pl.pallas_call(
        functools.partial(info_kernel, each),
        out_shape=shape_of(total, each * LANES),
        grid_spec=pltpu.PrefetchScalarGridSpec(
            num_scalar_prefetch=1,
            grid=(1,),
            in_specs=[
                full(rows),
                full(panel),
                pl.BlockSpec((total, None, group, LANES), lambda i, spot: (0, spot[4], 0, 0)),
                full(far) if far.ndim == 3 else half(far, 0),
                half(near, 1),
            ],
            out_specs=pl.BlockSpec((total, each * LANES), lambda i, spot: (0, 0)),
            scratch_shapes=[pltpu.VMEM((max(total, rows.shape[0]), each * LANES), jnp.float32)],
        ),
        compiler_params=params(),
        name="info_part",
    )(spot, rows, panel, prior, far, near)


def slab_kernel(count, spot_ref, inverse_ref, own_ref, other_ref, out_ref):
    total, width = own_ref.shape
    own_rows, chunk = total // count, width // LANES
    half = total // 2
    tile = (own_rows, LANES)
    row_ids = lax.broadcasted_iota(jnp.int32, tile, 0)
    lane_ids = lax.broadcasted_iota(jnp.int32, tile, 1)
    info = own_ref[...] + other_ref[...]
    for side in range(2):
        depth = (side + 1) * half
        slab = dot(inverse_ref[side * half : depth, :depth], info[:depth, :], 1, 0)
        for b in range(chunk):
            for e in range(count // 2):
                d = side * (count // 2) + e
                part = slab[e * own_rows : (e + 1) * own_rows, b * LANES : (b + 1) * LANES]
                kept = jnp.where(spot_ref[SPOTS + b] + lane_ids >= row_ids + d * own_rows, part, 0.0)
                out_ref[d, pl.ds(b, own_rows, stride=chunk), :] = kept


def slab_part(count, spot, inverse, own, other):
    total, width = own.shape
    return pl.pallas_call(
        functools.partial(slab_kernel, count),
        out_shape=shape_of(count, total // count * width // LANES, LANES),
        in_specs=[pl.BlockSpec(memory_space=pltpu.SMEM)] + [vmem_spec()] * 3,
        out_specs=vmem_spec(),
        compiler_params=params(),
        name="slab_part",
    )(spot, inverse, own, other)


def swapped(value, axis, bits):
    count = lax.axis_size(axis)
    return lax.ppermute(value, axis, [(i, i ^ bits) for i in range(count)])


def handed_on(value):
    return lax.ppermute(value, "section", [(0, 1)])


def z_panels(near):
    rows = lax.axis_size("row")
    return jnp.concatenate([near] + [swapped(near, "row", k) for k in range(2, rows, 2)], axis=0)


def prior_panels(near_prior):
    if lax.axis_size("col") == 2:
        return near_prior, swapped(near_prior, "col", 1)
    priors = lax.all_gather(near_prior, "col")
    return priors[0], priors[1]


def all_panels(near):
    rows, cols = lax.axis_size("row"), lax.axis_size("col")
    if cols == 2:
        order = [(i, i ^ 3) for i in range(rows * cols)]
        far = [swapped(near, "col", 1), lax.ppermute(near, ("row", "col"), order)]
        return [near, swapped(near, "row", 1)] + far
    both = lax.all_gather(near, "col")
    both = [both[0], both[1]]
    beside = [swapped(panel, "row", 1) for panel in both]
    return [both[0], beside[0], both[1], beside[1]]


def on_device(prior_root, observations, live_rows):
    total, cycles, _, width = prior_root.shape
    slots = observations.shape[1]
    rows, cols = lax.axis_size("row"), lax.axis_size("col")
    per = width // LANES
    blocks = cycles * per
    chunk = -(-blocks // rows)
    parts = 2 if chunk % GROUP == 0 else 1
    each = chunk // parts
    col, row, section = (lax.axis_index(axis) for axis in ("col", "row", "section"))
    group = min(GROUP, chunk * rows)

    def spot_of(part):
        first = row * chunk + part * each
        spot = [col if cols == 2 else 0, section, row, 0, first // group, first % group]
        spot += [((first + b) // per * cols + col) * width + (first + b) % per * LANES for b in range(each)]
        return jnp.stack([jnp.asarray(value, jnp.int32) for value in spot])

    def in_blocks(array):
        array = array.reshape(array.shape[0], blocks, LANES)
        return jnp.pad(array, ((0, 0), (0, chunk * rows - blocks), (0, 0)))

    spots = [spot_of(part) for part in range(parts)]
    prior = in_blocks(prior_root.reshape(total, -1)).reshape(total, -1, group, LANES)
    observed = in_blocks(observations.reshape(slots, -1)).reshape(slots, rows, chunk, LANES)
    live = lax.broadcasted_iota(jnp.int32, (slots, 1), 0) < live_rows[0, 0]
    near = jnp.where(live, observations[0, :, 0, 0, :], 0.0)
    same_side = [[2 * i + side for i in range(rows // 2)] for side in range(2)]

    def over(piece):
        return lax.all_to_all(piece, "row", 0, 0, axis_index_groups=same_side, tiled=True)

    near = z_panels(near)
    if parts > 1:
        crossing = pack(spots[0], observed, 1, each, [1])
        packed = pack(spots[0], observed, 0, each, [1, 0])
        packed, crossing, near = lax.optimization_barrier((packed, crossing, near))
        crossed = swapped(crossing, "row", 1)
    else:
        packed, near = lax.optimization_barrier((plain_pack(spots[0], observed), near))
    priors = prior_panels(prior_root[:, 0, 0, :])
    near, priors = lax.optimization_barrier((near, priors))
    panels = all_panels(near)
    first = over(packed)
    far = first[:, 0]
    far, _ = lax.optimization_barrier((far, panels))
    arrived = [(swapped(far, "row", 1), first)]
    if parts > 1:
        packed = pack(spots[0], observed, 1, each, [0], crossed)
        packed, panels = lax.optimization_barrier((packed, panels))
    rows_panel, prior_panel, gram = panel_gram(rows, spots[0], panels, *priors)
    other_gram = handed_on(gram)
    if parts > 1:
        packed, first = lax.optimization_barrier((packed, first))
        second = over(packed)
        arrived.append((second, second))
    inverse = factor(gram, other_gram)
    rows_panel, inverse = lax.optimization_barrier((rows_panel, inverse))
    out = jnp.zeros((total // rows, rows, parts, each, LANES), jnp.float32)
    for part, (far, near) in enumerate(arrived):
        info = info_part(each, spots[part], rows_panel, prior_panel, prior, far, near)
        slab = slab_part(rows, spots[part], inverse, info, handed_on(info))
        slab = lax.all_to_all(slab, "row", 0, 0, tiled=True)
        slab = slab.reshape(rows, total // rows, each, LANES).transpose(1, 0, 2, 3)
        out = out.at[:, :, part].set(slab)
    out = out.reshape(total // rows, rows * chunk, LANES)[:, :blocks]
    return out.reshape(1, total // rows, cycles, 1, width)


def solution(mesh):
    placed = (
        P(None, None, "col", None),
        P("section", "row", None, "col", None),
        P("section", "row"),
    )
    return jax.shard_map(
        on_device,
        mesh=mesh,
        in_specs=placed,
        out_specs=P("section", "row", None, "col", None),
        check_vma=False,
    )
```

profile of v0, /device:TPU:0, one launch (start us, length us, event | category | flops | bytes accessed | tf_op | source)
XLA Modules:
  0.0 192.7 jit_solution(9503428122452604388)
XLA Ops:
  0.7 0.9 slice.68
  1.6 0.1 fusion
  1.7 5.1 %collective-permute-start.2 = (f32[128,256]{1,0:T(8,128)S(1)}, f32[128,256]{1,0:T(8,128)S(1)}, u32[]{:S(2)}, u32[]{:S(2)}) collective-permute-start(f32[128,256]{1,0:T(8,128)S(1)} %fusion), channel_id=1, source_target_pairs={{0,12},{2,14},{4,8},{6,10},{8,4},{10,6},{12,0},{14,2},{1,13},{3,15... | collective-permute-start | bytes 393224 | tf_op jit(solution)/shard_map/ppermute | solution.py:318
  6.8 0.6 collective-permute-start
  7.4 0.6 stack.63.spot_ref
  8.0 4.3 %pack.4 = f32[4,512,128]{2,1,0:T(8,128)} custom-call(s32[10]{0:T(128)} %stack.63.spot_ref, f32[128,8,8,128]{3,2,1,0:T(8,128)} %bitcast.41), custom_call_target="tpu_custom_call" | custom-call | tf_op jit(solution)/shard_map/pack/pallas_call | solution.py:227
  12.3 5.0 %pack.3 = f32[4,2,512,128]{3,2,1,0:T(8,128)} custom-call(s32[10]{0:T(128)} %stack.63.spot_ref, f32[128,8,8,128]{3,2,1,0:T(8,128)} %bitcast.42, f32[128,8,8,128]{3,2,1,0:T(8,128)} %bitcast.43), custom_call_target="tpu_custom_call" | custom-call | tf_op jit(solution)/shard_map/pack/pallas_call | solution.py:227
  17.3 0.5 collective-permute-done.1
  17.9 4.6 %all-to-all-start = ((f32[4,2,512,128]{3,2,1,0:T(8,128)}), f32[4,2,512,128]{3,2,1,0:T(8,128)S(1)}, u32[]{:S(2)}, u32[]{:S(2)}) async-start(f32[4,2,512,128]{3,2,1,0:T(8,128)} %pack.3), calls=%async_computation | async-start | bytes 4194304 | tf_op jit(solution)/shard_map/all_to_all | solution.py:379
  22.6 1.6 collective-permute-start.4
  24.2 1.5 collective-permute-start.3
  25.7 9.5 %collective-permute-done.4.refs_4_ = f32[512,256]{1,0:T(8,128)S(1)} collective-permute-done((f32[512,256]{1,0:T(8,128)S(1)}, f32[512,256]{1,0:T(8,128)S(1)}, u32[]{:S(2)}, u32[]{:S(2)}) %collective-permute-start.4) | collective-permute-done | bytes 524320 | tf_op jit(solution)/shard_map/ppermute | solution.py:318
  35.2 2.4 %collective-permute-start.7 = (f32[512,256]{1,0:T(8,128)S(1)}, f32[512,256]{1,0:T(8,128)S(1)}, u32[]{:S(2)}, u32[]{:S(2)}) collective-permute-start(f32[512,256]{1,0:T(8,128)S(1)} %pad_maximum_fusion.1.near_ref), channel_id=1, source_target_pairs={{0,3},{1,2},{2,1},{3,0},{4,7},{5,6},{6,5},{7,4},{8,11},{9,10},{10,... | collective-permute-start | bytes 1572872 | tf_op jit(solution)/shard_map/ppermute | solution.py:341
  37.7 0.5 collective-permute-start.6
  38.2 0.5 collective-permute-start.5
  38.7 11.6 %collective-permute-done.3.refs_0_ = f32[4,512,128]{2,1,0:T(8,128)S(1)} collective-permute-done((f32[4,512,128]{2,1,0:T(8,128)S(1)}, f32[4,512,128]{2,1,0:T(8,128)S(1)}, u32[]{:S(2)}, u32[]{:S(2)}) %collective-permute-start.3) | collective-permute-done | bytes 1048608 | tf_op jit(solution)/shard_map/ppermute | solution.py:318
  50.3 1.0 copy-done.9
  51.3 4.7 %pack.5 = f32[4,2,512,128]{3,2,1,0:T(8,128)} custom-call(s32[10]{0:T(128)} %stack.63.spot_ref, f32[4,512,128]{2,1,0:T(8,128)} %copy-done.9, f32[128,8,8,128]{3,2,1,0:T(8,128)} %bitcast.44), custom_call_target="tpu_custom_call" | custom-call | tf_op jit(solution)/shard_map/pack/pallas_call | solution.py:227
  56.0 6.3 %collective-permute-done.7.refs_2_ = f32[512,256]{1,0:T(8,128)S(1)} collective-permute-done((f32[512,256]{1,0:T(8,128)S(1)}, f32[512,256]{1,0:T(8,128)S(1)}, u32[]{:S(2)}, u32[]{:S(2)}) %collective-permute-start.7) | collective-permute-done | bytes 524320 | tf_op jit(solution)/shard_map/ppermute | solution.py:341
  62.3 0.8 copy-done.12
  63.1 0.8 copy-done.13
  64.0 6.4 %collective-permute-done.5.refs_0_ = f32[512,256]{1,0:T(8,128)} collective-permute-done((f32[512,256]{1,0:T(8,128)S(1)}, f32[512,256]{1,0:T(8,128)}, u32[]{:S(2)}, u32[]{:S(2)}) %collective-permute-start.5) | collective-permute-done | bytes 524320 | tf_op jit(solution)/shard_map/ppermute | solution.py:318
  70.4 1.3 copy-done.1
  71.7 4.8 %all-to-all-start.2 = ((f32[4,2,512,128]{3,2,1,0:T(8,128)}), f32[4,2,512,128]{3,2,1,0:T(8,128)S(1)}, u32[]{:S(2)}, u32[]{:S(2)}) async-start(f32[4,2,512,128]{3,2,1,0:T(8,128)} %pack.5), calls=%async_computation.2 | async-start | bytes 4194304 | tf_op jit(solution)/shard_map/all_to_all | solution.py:379
  76.5 6.9 %panel_gram.1 = (f32[1024,512]{1,0:T(8,128)}, f32[512,512]{1,0:T(8,128)}, f32[512,512]{1,0:T(8,128)}) custom-call(s32[10]{0:T(128)} %stack.63.spot_ref, f32[512,256]{1,0:T(8,128)} %copy-done.3, f32[512,256]{1,0:T(8,128)} %collective-permute-done.5.refs_0_, f32[512,256]{1,0:T(8,128)} %copy-done.13, f32[512,256]{1,0:T(8,128)} %copy-done.12, ...), custom_call_target="tpu_custom_call" | custom-call | tf_op jit(solution)/shard_map/panel_gram/pallas_call | solution.py:179
  83.3 1.5 collective-permute-start.8
  85.0 1.6 collective-permute-start.9
  86.5 0.6 collective-permute-done.8.other_ref
  87.1 1.1 copy-done.5
  88.2 18.8 %factor.1.inverse_ref = f32[512,512]{1,0:T(8,128)} custom-call(f32[512,512]{1,0:T(8,128)} %get-tuple-element.57.own_ref, f32[512,512]{1,0:T(8,128)} %copy-done.5), custom_call_target="tpu_custom_call" | custom-call | tf_op jit(solution)/shard_map/factor/pallas_call | solution.py:133
  107.0 0.5 collective-permute-done.9.far_ref
  107.5 1.1 copy-done.10
  108.5 10.1 %info_part.2.own_ref = f32[512,512]{1,0:T(8,128)} custom-call(s32[10]{0:T(128)} %stack.63.spot_ref, f32[1024,512]{1,0:T(8,128)} %get-tuple-element.59.rows_ref, f32[512,512]{1,0:T(8,128)} %get-tuple-element.60.panel_ref, f32[512,8,8,128]{3,2,1,0:T(8,128)} %bitcast.39, f32[4,512,128]{2,1,0:T(8,128)} %copy-done.10, f32[4,2,512,128]{3,2,1,0:T(8,128)} %copy-done.1), custom_call_target="tpu_custom_call" | custom-call | tf_op jit(solution)/shard_map/info_part/pallas_call | solution.py:264
  118.7 1.9 collective-permute-start.10
  120.6 2.4 %collective-permute-done.10.other_ref = f32[512,512]{1,0:T(8,128)S(1)} collective-permute-done((f32[512,512]{1,0:T(8,128)}, f32[512,512]{1,0:T(8,128)S(1)}, u32[]{:S(2)}, u32[]{:S(2)}) %collective-permute-start.10) | collective-permute-done | bytes 1048608 | tf_op jit(solution)/shard_map/ppermute | solution.py:322
  123.0 1.0 copy-done.7
  124.0 4.4 %slab_part.2 = f32[8,256,128]{2,1,0:T(8,128)} custom-call(s32[10]{0:T(128)} %stack.63.spot_ref, f32[512,512]{1,0:T(8,128)} %factor.1.inverse_ref, f32[512,512]{1,0:T(8,128)} %info_part.2.own_ref, f32[512,512]{1,0:T(8,128)} %copy-done.7), custom_call_target="tpu_custom_call" | custom-call | tf_op jit(solution)/shard_map/slab_part/pallas_call | solution.py:306
  128.3 6.0 %all-to-all-start.1 = ((f32[8,256,128]{2,1,0:T(8,128)}), f32[8,256,128]{2,1,0:T(8,128)S(1)}, u32[]{:S(2)}, u32[]{:S(2)}) async-start(f32[8,256,128]{2,1,0:T(8,128)} %slab_part.2), calls=%async_computation.1 | async-start | bytes 2097152 | tf_op jit(solution)/shard_map/all_to_all | solution.py:411
  134.4 0.6 stack.70.spot_ref
  135.0 9.9 %info_part.3.own_ref = f32[512,512]{1,0:T(8,128)} custom-call(s32[10]{0:T(128)} %stack.70.spot_ref, f32[1024,512]{1,0:T(8,128)} %get-tuple-element.59.rows_ref, f32[512,512]{1,0:T(8,128)} %get-tuple-element.60.panel_ref, f32[512,8,8,128]{3,2,1,0:T(8,128)} %bitcast.40, f32[4,2,512,128]{3,2,1,0:T(8,128)} %copy-done, f32[4,2,512,128]{3,2,1,0:T(8,128)} %copy-done), custom_call_target="tpu_custom_call" | custom-call | tf_op jit(solution)/shard_map/info_part/pallas_call | solution.py:264
  144.9 2.0 %collective-permute-start.11 = (f32[512,512]{1,0:T(8,128)}, f32[512,512]{1,0:T(8,128)S(1)}, u32[]{:S(2)}, u32[]{:S(2)}) collective-permute-start(f32[512,512]{1,0:T(8,128)} %info_part.3.own_ref), channel_id=1, source_target_pairs={{0,16},{1,17},{2,18},{3,19},{4,20},{5,21},{6,22},{7,23},{8,24},{9,... | collective-permute-start | bytes 3145736 | tf_op jit(solution)/shard_map/ppermute | solution.py:322
  147.0 2.4 %collective-permute-done.11.other_ref = f32[512,512]{1,0:T(8,128)S(1)} collective-permute-done((f32[512,512]{1,0:T(8,128)}, f32[512,512]{1,0:T(8,128)S(1)}, u32[]{:S(2)}, u32[]{:S(2)}) %collective-permute-start.11) | collective-permute-done | bytes 1048608 | tf_op jit(solution)/shard_map/ppermute | solution.py:322
  149.4 1.0 copy-done.6
  150.4 4.4 %slab_part.3 = f32[8,256,128]{2,1,0:T(8,128)} custom-call(s32[10]{0:T(128)} %stack.70.spot_ref, f32[512,512]{1,0:T(8,128)} %factor.1.inverse_ref, f32[512,512]{1,0:T(8,128)} %info_part.3.own_ref, f32[512,512]{1,0:T(8,128)} %copy-done.6), custom_call_target="tpu_custom_call" | custom-call | tf_op jit(solution)/shard_map/slab_part/pallas_call | solution.py:306
  154.8 5.9 %all-to-all-done.1 = f32[8,256,128]{2,1,0:T(8,128)S(1)} async-done(((f32[8,256,128]{2,1,0:T(8,128)}), f32[8,256,128]{2,1,0:T(8,128)S(1)}, u32[]{:S(2)}, u32[]{:S(2)}) %all-to-all-start.1) | async-done | bytes 1048608 | tf_op jit(solution)/shard_map/all_to_all | solution.py:411
  160.7 29.5 %all_to_all.20 = f32[8,256,128]{2,1,0:T(8,128)S(1)} all-to-all(f32[8,256,128]{2,1,0:T(8,128)} %slab_part.3), channel_id=1, replica_groups=mesh['section'=2,'row'=8,'col'=2] {'row'}, dimensions={0} | all-to-all | bytes 2097152 | tf_op jit(solution)/shard_map/all_to_all | solution.py:411
  190.2 0.5 pad_maximum_fusion
  190.7 1.9 copy.6
  (32 shorter events, 0.2 us)
Async XLA Ops:
  1.7 15.6 %collective-permute-start.2 = (f32[128,256]{1,0:T(8,128)S(1)}, f32[128,256]{1,0:T(8,128)S(1)}, u32[]{:S(2)}, u32[]{:S(2)}) collective-permute-start(f32[128,256]{1,0:T(8,128)S(1)} %fusion), channel_id=1, source_target_pairs={{0,12},{2,14},{4,8},{6,10},{8,4},{10,6},{12,0},{14,2},{1,13},{3,15... | collective-permute-start | bytes 393224 | tf_op jit(solution)/shard_map/ppermute | solution.py:318
  6.8 11.1 %collective-permute-start.1 = (f32[128,256]{1,0:T(8,128)S(1)}, f32[128,256]{1,0:T(8,128)S(1)}, u32[]{:S(2)}, u32[]{:S(2)}) collective-permute-start(f32[128,256]{1,0:T(8,128)S(1)} %fusion), channel_id=1, source_target_pairs={{0,8},{2,10},{4,12},{6,14},{8,0},{10,2},{12,4},{14,6},{1,9},{3,11}... | collective-permute-start | bytes 393224 | tf_op jit(solution)/shard_map/ppermute | solution.py:318
  6.8 11.1 %collective-permute-start = (f32[128,256]{1,0:T(8,128)S(1)}, f32[128,256]{1,0:T(8,128)S(1)}, u32[]{:S(2)}, u32[]{:S(2)}) collective-permute-start(f32[128,256]{1,0:T(8,128)S(1)} %fusion), channel_id=1, source_target_pairs={{0,4},{2,6},{4,0},{6,2},{8,12},{10,14},{12,8},{14,10},{1,5},{3,7},... | collective-permute-start | bytes 393224 | tf_op jit(solution)/shard_map/ppermute | solution.py:318
  17.9 20.3 %copy-start.3 = (f32[512,256]{1,0:T(8,128)}, f32[512,256]{1,0:T(8,128)S(1)}, u32[]{:S(2)}) copy-start(f32[512,256]{1,0:T(8,128)S(1)} %pad_maximum_fusion.1.near_ref) | copy-start | bytes 1572868
  17.9 4.6 %slice-start = ((f32[512,32,1,256]{3,2,1,0:T(1,128)}), f32[512,1,1,256]{3,2,1,0:T(1,128)S(1)}, s32[]{:S(2)}) async-start(f32[512,32,1,256]{3,2,1,0:T(1,128)} %param.7), calls=%async_computation.4 | async-start | bytes 1048576 | tf_op jit(solution)/shard_map/slice | solution.py:389
  17.9 52.5 %all-to-all-start = ((f32[4,2,512,128]{3,2,1,0:T(8,128)}), f32[4,2,512,128]{3,2,1,0:T(8,128)S(1)}, u32[]{:S(2)}, u32[]{:S(2)}) async-start(f32[4,2,512,128]{3,2,1,0:T(8,128)} %pack.3), calls=%async_computation | async-start | bytes 4194304 | tf_op jit(solution)/shard_map/all_to_all | solution.py:379
  22.6 1.6 copy-start.8
  22.6 16.1 %copy-start.4 = (f32[512,1,1,256]{3,0,2,1:T(8,128)}, f32[512,1,1,256]{3,0,2,1:T(8,128)S(1)}, u32[]{:S(2)}) copy-start(f32[512,1,1,256]{3,0,2,1:T(8,128)S(1)} %copy.13) | copy-start | bytes 1572868
  22.6 12.6 %collective-permute-start.4 = (f32[512,256]{1,0:T(8,128)S(1)}, f32[512,256]{1,0:T(8,128)S(1)}, u32[]{:S(2)}, u32[]{:S(2)}) collective-permute-start(f32[512,256]{1,0:T(8,128)S(1)} %bitcast.47), channel_id=1, source_target_pairs={{0,1},{1,0},{2,3},{3,2},{4,5},{5,4},{6,7},{7,6},{8,9},{9,8},{10,11... | collective-permute-start | bytes 1572872 | tf_op jit(solution)/shard_map/ppermute | solution.py:318
  24.2 26.1 %collective-permute-start.3 = (f32[4,512,128]{2,1,0:T(8,128)S(1)}, f32[4,512,128]{2,1,0:T(8,128)S(1)}, u32[]{:S(2)}, u32[]{:S(2)}) collective-permute-start(f32[4,512,128]{2,1,0:T(8,128)S(1)} %copy-done.8), channel_id=1, source_target_pairs={{0,2},{2,0},{4,6},{6,4},{8,10},{10,8},{12,14},{14,12},{1,3},{3,1},... | collective-permute-start | bytes 3145736 | tf_op jit(solution)/shard_map/ppermute | solution.py:318
  35.2 3.5 %copy-start.11 = (f32[512,256]{1,0:T(8,128)}, f32[512,256]{1,0:T(8,128)S(1)}, u32[]{:S(2)}) copy-start(f32[512,256]{1,0:T(8,128)S(1)} %collective-permute-done.4.refs_4_) | copy-start | bytes 1572868
  35.2 27.1 %collective-permute-start.7 = (f32[512,256]{1,0:T(8,128)S(1)}, f32[512,256]{1,0:T(8,128)S(1)}, u32[]{:S(2)}, u32[]{:S(2)}) collective-permute-start(f32[512,256]{1,0:T(8,128)S(1)} %pad_maximum_fusion.1.near_ref), channel_id=1, source_target_pairs={{0,3},{1,2},{2,1},{3,0},{4,7},{5,6},{6,5},{7,4},{8,11},{9,10},{10,... | collective-permute-start | bytes 1572872 | tf_op jit(solution)/shard_map/ppermute | solution.py:341
  37.7 24.6 %collective-permute-start.6 = (f32[512,256]{1,0:T(8,128)S(1)}, f32[512,256]{1,0:T(8,128)S(1)}, u32[]{:S(2)}, u32[]{:S(2)}) collective-permute-start(f32[512,256]{1,0:T(8,128)S(1)} %pad_maximum_fusion.1.near_ref), channel_id=1, source_target_pairs={{0,1},{1,0},{2,3},{3,2},{4,5},{5,4},{6,7},{7,6},{8,9},{9,8},{10,11... | collective-permute-start | bytes 1572872 | tf_op jit(solution)/shard_map/ppermute | solution.py:318
  38.2 32.2 %collective-permute-start.5 = (f32[512,256]{1,0:T(8,128)S(1)}, f32[512,256]{1,0:T(8,128)}, u32[]{:S(2)}, u32[]{:S(2)}) collective-permute-start(f32[512,256]{1,0:T(8,128)S(1)} %pad_maximum_fusion.1.near_ref), channel_id=1, source_target_pairs={{0,2},{2,0},{4,6},{6,4},{8,10},{10,8},{12,14},{14,12},{1,3},{3,1},... | collective-permute-start | bytes 1572872 | tf_op jit(solution)/shard_map/ppermute | solution.py:318
  50.3 1.0 copy-start.9
  62.3 0.8 copy-start.12
  63.1 0.8 copy-start.13
  70.4 1.3 copy-start.1
  71.7 56.6 %all-to-all-start.2 = ((f32[4,2,512,128]{3,2,1,0:T(8,128)}), f32[4,2,512,128]{3,2,1,0:T(8,128)S(1)}, u32[]{:S(2)}, u32[]{:S(2)}) async-start(f32[4,2,512,128]{3,2,1,0:T(8,128)} %pack.5), calls=%async_computation.2 | async-start | bytes 4194304 | tf_op jit(solution)/shard_map/all_to_all | solution.py:379
  76.5 8.4 %copy-start.2 = (f32[4,2,512,128]{3,2,1,0:T(8,128)S(1)}, f32[4,2,512,128]{3,2,1,0:T(8,128)}, u32[]{:S(2)}) copy-start(f32[4,2,512,128]{3,2,1,0:T(8,128)} %copy-done.1) | copy-start | bytes 6291460
  83.3 3.8 %collective-permute-start.8 = (f32[512,512]{1,0:T(8,128)}, f32[512,512]{1,0:T(8,128)S(1)}, u32[]{:S(2)}, u32[]{:S(2)}) collective-permute-start(f32[512,512]{1,0:T(8,128)} %get-tuple-element.57.own_ref), channel_id=1, source_target_pairs={{0,16},{1,17},{2,18},{3,19},{4,20},{5,21},{6,22},{7,23},{8,24},{9,... | collective-permute-start | bytes 3145736 | tf_op jit(solution)/shard_map/ppermute | solution.py:322
  85.0 22.5 %collective-permute-start.9 = (f32[4,512,128]{2,1,0:T(8,128)S(1)}, f32[4,512,128]{2,1,0:T(8,128)S(1)}, u32[]{:S(2)}, u32[]{:S(2)}) collective-permute-start(f32[4,512,128]{2,1,0:T(8,128)S(1)} %slice_bitcast_fusion), channel_id=1, source_target_pairs={{0,2},{2,0},{4,6},{6,4},{8,10},{10,8},{12,14},{14,12},{1,3},{3,1},... | collective-permute-start | bytes 3145736 | tf_op jit(solution)/shard_map/ppermute | solution.py:318
  87.1 1.1 copy-start.5
  107.5 1.1 copy-start.10
  118.7 4.3 %collective-permute-start.10 = (f32[512,512]{1,0:T(8,128)}, f32[512,512]{1,0:T(8,128)S(1)}, u32[]{:S(2)}, u32[]{:S(2)}) collective-permute-start(f32[512,512]{1,0:T(8,128)} %info_part.2.own_ref), channel_id=1, source_target_pairs={{0,16},{1,17},{2,18},{3,19},{4,20},{5,21},{6,22},{7,23},{8,24},{9,... | collective-permute-start | bytes 3145736 | tf_op jit(solution)/shard_map/ppermute | solution.py:322
  123.0 1.0 copy-start.7
  128.3 6.7 %copy-start = (f32[4,2,512,128]{3,2,1,0:T(8,128)}, f32[4,2,512,128]{3,2,1,0:T(8,128)S(1)}, u32[]{:S(2)}) copy-start(f32[4,2,512,128]{3,2,1,0:T(8,128)S(1)} %all-to-all-done.2.far_ref.near_ref) | copy-start | bytes 6291460
  128.3 32.3 %all-to-all-start.1 = ((f32[8,256,128]{2,1,0:T(8,128)}), f32[8,256,128]{2,1,0:T(8,128)S(1)}, u32[]{:S(2)}, u32[]{:S(2)}) async-start(f32[8,256,128]{2,1,0:T(8,128)} %slab_part.2), calls=%async_computation.1 | async-start | bytes 2097152 | tf_op jit(solution)/shard_map/all_to_all | solution.py:411
  144.9 4.5 %collective-permute-start.11 = (f32[512,512]{1,0:T(8,128)}, f32[512,512]{1,0:T(8,128)S(1)}, u32[]{:S(2)}, u32[]{:S(2)}) collective-permute-start(f32[512,512]{1,0:T(8,128)} %info_part.3.own_ref), channel_id=1, source_target_pairs={{0,16},{1,17},{2,18},{3,19},{4,20},{5,21},{6,22},{7,23},{8,24},{9,... | collective-permute-start | bytes 3145736 | tf_op jit(solution)/shard_map/ppermute | solution.py:322
  149.4 1.0 copy-start.6
where the time goes:
time: 193 us
  Pallas kernels  68.5 us (35%)
  waiting for transfers between devices  46.2 us (24%)
  starting transfers between devices  34.8 us (18%)
  blocking collectives  29.5 us (15%)
  local copies, waits for them, and re-layouts  12.3 us (6%)
    all_to_all x1, blocking collectives, on_device(): slab = lax.all_to_all(slab, 'row', 0, 0, tiled=True)  29.5 us
    ppermute x8, waiting for transfers between devices, swapped(): return lax.ppermute(value, axis, [(i, i ^ bits) for i in range(count)])  28.5 us
    pallas_call x2, Pallas kernels, info_part(): pl.pallas_call(functools.partial(info_kernel, each), out_shape=shape_of(t...  20.1 us
    pallas_call x1, Pallas kernels, factor(): pl.pallas_call(factor_kernel, out_shape=shape_of(size, size), in_specs=[v...  18.8 us
    pallas_call x3, Pallas kernels, pack(): pl.pallas_call(functools.partial(pack_kernel, part * each, each, swapped_...  14 us
    ppermute x8, starting transfers between devices, swapped(): return lax.ppermute(value, axis, [(i, i ^ bits) for i in range(count)])  11.4 us
    all_to_all x2, starting transfers between devices, over(): lax.all_to_all(piece, 'row', 0, 0, axis_index_groups=same_side, tiled=True)  9.39 us
    pallas_call x2, Pallas kernels, slab_part(): pl.pallas_call(functools.partial(slab_kernel, count), out_shape=shape_of(...  8.77 us
  transfers between devices with their start and end apart: 15, of which 10 were waited for; matrix products, arithmetic and copies ran while one was open for 1% of the time, Pallas kernels for 36%

commit v1 on v0

--- a/solution.py
+++ b/solution.py
@@ -144,15 +144,56 @@
     )(own, other)
 
 
-def panel_kernel(count, spot_ref, near_ref, *refs):
-    near_prior, far_prior, rows_ref, prior_ref, gram_ref = refs[-5:]
-    parts = refs[:-5]
+def prior_kernel(chunk, spot_ref, near_prior, far_prior, blocks_ref, info_ref, gram_ref, panel, work):
+    total, group = blocks_ref.shape[0], blocks_ref.shape[1]
     width = near_prior.shape[1]
     col, section = spot_ref[0], spot_ref[1]
     near_at = pl.ds(pl.multiple_of(col * width, width), width)
     far_at = pl.ds(pl.multiple_of((1 - col) * width, width), width)
+    keep = (section == 0).astype(jnp.float32)
+    panel[:, near_at] = near_prior[...] * keep
+    panel[:, far_at] = far_prior[...] * keep
+    upper = panel[:width, :]
+    gram_ref[:width, :] = dot(upper[:, :width], upper, 0, 0)
+    corner = panel[:, width:]
+    gram_ref[width:, width:] = dot(corner, corner, 0, 0)
+    gram_ref[width:, :width] = jnp.zeros((width, width), jnp.float32)
+    gather_blocks(blocks_ref.reshape(total * group, LANES), spot_ref[5], total, group, chunk, work, 0)
+    info_ref[...] = dot(panel[...], work[...], 0, 0)
+
+
+def prior_part(chunk, spot, near_prior, far_prior, prior):
+    total, _, group, _ = prior.shape
+    full = lambda array: pl.BlockSpec(array.shape, lambda i, spot: (0,) * array.ndim)
+    out = (shape_of(total, chunk * LANES), shape_of(total, total))
+    return pl.pallas_call(
+        functools.partial(prior_kernel, chunk),
+        out_shape=out,
+        grid_spec=pltpu.PrefetchScalarGridSpec(
+            num_scalar_prefetch=1,
+            grid=(1,),
+            in_specs=[
+                full(near_prior),
+                full(far_prior),
+                pl.BlockSpec((total, None, group, LANES), lambda i, spot: (0, spot[4], 0, 0)),
+            ],
+            out_specs=[full(array) for array in out],
+            scratch_shapes=[
+                pltpu.VMEM((total, total), jnp.float32),
+                pltpu.VMEM((total, chunk * LANES), jnp.float32),
+            ],
+        ),
+        compiler_params=params(),
+        name="prior_part",
+    )(spot, near_prior, far_prior, prior)
+
+
+def panel_kernel(count, spot_ref, near_ref, near_next, far_here, far_next, prior_ref, rows_ref, gram_ref):
+    width = near_ref.shape[1]
+    col = spot_ref[0]
+    near_at = pl.ds(pl.multiple_of(col * width, width), width)
+    far_at = pl.ds(pl.multiple_of((1 - col) * width, width), width)
     slots = near_ref.shape[0] * 2 // count
-    near_next, far_here, far_next = parts
     pair = spot_ref[2] // 2
     for i in range(count // 2):
         here, beside = (pl.ds(((pair ^ i) + side) * slots, slots) for side in (0, count // 2))
@@ -161,38 +202,29 @@
         rows_ref[beside, near_at] = near_next[piece]
         rows_ref[here, far_at] = far_here[piece]
         rows_ref[beside, far_at] = far_next[piece]
-    keep = (section == 0).astype(jnp.float32)
-    prior_ref[:, near_at] = near_prior[...] * keep
-    prior_ref[:, far_at] = far_prior[...] * keep
-    left = rows_ref[:, :width]
     right = rows_ref[:, width:]
-    prior = prior_ref[:width, :]
-    gram_ref[:width, :] = dot(left, rows_ref[...], 0, 0) + dot(prior[:, :width], prior, 0, 0)
-    corner = prior_ref[:, width:]
-    gram_ref[width:, width:] = dot(right, right, 0, 0) + dot(corner, corner, 0, 0)
+    gram_ref[:width, :] = prior_ref[:width, :] + dot(rows_ref[:, :width], rows_ref[...], 0, 0)
+    gram_ref[width:, width:] = prior_ref[width:, width:] + dot(right, right, 0, 0)
     gram_ref[width:, :width] = jnp.zeros((width, width), jnp.float32)
 
 
-def panel_gram(count, spot, parts, near_prior, far_prior):
-    slots = parts[0].shape[0] * 2 // count
-    total, width = near_prior.shape
+def panel_gram(count, spot, parts, prior_gram):
+    slots, total = parts[0].shape[0] * 2 // count, prior_gram.shape[0]
     return pl.pallas_call(
         functools.partial(panel_kernel, count),
-        out_shape=(
-            shape_of(count * slots, 2 * width),
-            shape_of(total, 2 * width),
-            shape_of(total, total),
-        ),
-        in_specs=[pl.BlockSpec(memory_space=pltpu.SMEM)] + [vmem_spec()] * 6,
-        out_specs=(vmem_spec(),) * 3,
+        out_shape=(shape_of(count * slots, total), shape_of(total, total)),
+        in_specs=[pl.BlockSpec(memory_space=pltpu.SMEM)] + [vmem_spec()] * 5,
+        out_specs=(vmem_spec(),) * 2,
         compiler_params=params(),
         name="panel_gram",
-    )(spot, *parts, near_prior, far_prior)
+    )(spot, *parts, prior_gram)
 
 
 def gather_blocks(ref, first, rows, stride, blocks, work, at):
     for b in range(blocks):
-        work[at : at + rows, b * LANES : (b + 1) * LANES] = ref[pl.ds(first + b, rows, stride=stride), :]
+        work[pl.ds(at, rows), b * LANES : (b + 1) * LANES] = ref[
+            pl.ds(first + b, rows, stride=stride), :
+        ]
 
 
 def pack_kernel(first, each, joined, spot_ref, *refs):
@@ -242,25 +274,21 @@
     return jnp.stack(sides, axis=1).reshape(rows // 2, 2, slots * chunk, LANES)
 
 
-def info_kernel(each, spot_ref, rows_ref, panel_ref, prior_ref, far_ref, near_ref, out_ref, work):
-    total, group = prior_ref.shape[0], prior_ref.shape[1]
+def info_kernel(each, spot_ref, rows_ref, prior_ref, far_ref, near_ref, out_ref, work):
     count, pairs = rows_ref.shape[0], far_ref.shape[0]
     slots = count // 2 // pairs
-    flat = prior_ref.reshape(total * group, LANES)
-    gather_blocks(flat, spot_ref[5], total, group, each, work, 0)
-    part = dot(panel_ref[...], work[:total, :], 0, 0)
     for i in range(pairs):
         gather_blocks(near_ref.at[i], 0, slots, each, each, work, i * slots)
         gather_blocks(far_ref.at[i], 0, slots, each, each, work, count // 2 + i * slots)
-    out_ref[...] = part + dot(rows_ref[...], work[:count, :], 0, 0)
-
-
-def info_part(each, spot, rows, panel, prior, far, near):
-    total, _, group, _ = prior.shape
-    full = lambda array: pl.BlockSpec(array.shape, lambda i, spot: (0,) * array.ndim)
+    out_ref[...] = prior_ref[...] + dot(rows_ref[...], work[...], 0, 0)
+
+
+def info_part(part, each, spot, rows, prior_info, far, near):
+    total = prior_info.shape[0]
     half = lambda array, at: pl.BlockSpec(
         (array.shape[0], None) + array.shape[2:], lambda i, spot: (0, at, 0, 0)
     )
+    full = lambda array: pl.BlockSpec(array.shape, lambda i, spot: (0,) * array.ndim)
     return pl.pallas_call(
         functools.partial(info_kernel, each),
         out_shape=shape_of(total, each * LANES),
@@ -269,17 +297,16 @@
             grid=(1,),
             in_specs=[
                 full(rows),
-                full(panel),
-                pl.BlockSpec((total, None, group, LANES), lambda i, spot: (0, spot[4], 0, 0)),
+                pl.BlockSpec((total, each * LANES), lambda i, spot: (0, part)),
                 full(far) if far.ndim == 3 else half(far, 0),
                 half(near, 1),
             ],
             out_specs=pl.BlockSpec((total, each * LANES), lambda i, spot: (0, 0)),
-            scratch_shapes=[pltpu.VMEM((max(total, rows.shape[0]), each * LANES), jnp.float32)],
+            scratch_shapes=[pltpu.VMEM((rows.shape[0], each * LANES), jnp.float32)],
         ),
         compiler_params=params(),
         name="info_part",
-    )(spot, rows, panel, prior, far, near)
+    )(spot, rows, prior_info, far, near)
 
 
 def slab_kernel(count, spot_ref, inverse_ref, own_ref, other_ref, out_ref):
@@ -379,24 +406,26 @@
         return lax.all_to_all(piece, "row", 0, 0, axis_index_groups=same_side, tiled=True)
 
     near = z_panels(near)
+    priors = prior_panels(prior_root[:, 0, 0, :])
     if parts > 1:
         crossing = pack(spots[0], observed, 1, each, [1])
         packed = pack(spots[0], observed, 0, each, [1, 0])
         packed, crossing, near = lax.optimization_barrier((packed, crossing, near))
         crossed = swapped(crossing, "row", 1)
+        near, priors = lax.optimization_barrier((near, priors))
     else:
         packed, near = lax.optimization_barrier((plain_pack(spots[0], observed), near))
-    priors = prior_panels(prior_root[:, 0, 0, :])
-    near, priors = lax.optimization_barrier((near, priors))
     panels = all_panels(near)
     first = over(packed)
     far = first[:, 0]
     far, _ = lax.optimization_barrier((far, panels))
     arrived = [(swapped(far, "row", 1), first)]
+    prior_info, prior_gram = prior_part(chunk, spots[0], *priors, prior)
     if parts > 1:
+        observed, prior_gram = lax.optimization_barrier((observed, prior_gram))
         packed = pack(spots[0], observed, 1, each, [0], crossed)
         packed, panels = lax.optimization_barrier((packed, panels))
-    rows_panel, prior_panel, gram = panel_gram(rows, spots[0], panels, *priors)
+    rows_panel, gram = panel_gram(rows, spots[0], panels, prior_gram)
     other_gram = handed_on(gram)
     if parts > 1:
         packed, first = lax.optimization_barrier((packed, first))
@@ -406,8 +435,11 @@
     rows_panel, inverse = lax.optimization_barrier((rows_panel, inverse))
     out = jnp.zeros((total // rows, rows, parts, each, LANES), jnp.float32)
     for part, (far, near) in enumerate(arrived):
-        info = info_part(each, spots[part], rows_panel, prior_panel, prior, far, near)
-        slab = slab_part(rows, spots[part], inverse, info, handed_on(info))
+        if part:
+            rows_panel, other = lax.optimization_barrier((rows_panel, other))
+        info = info_part(part, each, spots[part], rows_panel, prior_info, far, near)
+        other = handed_on(info)
+        slab = slab_part(rows, spots[part], inverse, info, other)
         slab = lax.all_to_all(slab, "row", 0, 0, tiled=True)
         slab = slab.reshape(rows, total // rows, each, LANES).transpose(1, 0, 2, 3)
         out = out.at[:, :, part].set(slab)

time: 193 us -> 190 us (0.984)
  waiting for transfers between devices: 46.2 us -> 39.7 us
  Pallas kernels: 68.5 us -> 71.9 us
    pallas_call x0 -> x1, Pallas kernels: none -> 8.77 us  [prior_part(): pl.pallas_call(functools.partial(prior_kernel, chunk), out_shape=out, gri...]
    ppermute x8, waiting for transfers between devices: 28.5 us -> 19.9 us  [swapped(): return lax.ppermute(value, axis, [(i, i ^ bits) for i in range(count)])]
    pallas_call x2, Pallas kernels: 20.1 us -> 15.6 us  [info_part(): pl.pallas_call(functools.partial(info_kernel, each), out_shape=shape_of(t...]
    all_to_all x1, waiting for transfers between devices: 5.91 us -> 8.21 us  [on_device(): slab = lax.all_to_all(slab, 'row', 0, 0, tiled=True)]
  transfers between devices with their start and end apart: 15 -> 15, of which waited for: 10 -> 10; matrix products, arithmetic and copies ran while one was open for 1% -> 1% of each run, Pallas kernels for 36% -> 38%
where the time goes in v1:
time: 190 us
  Pallas kernels  71.9 us (38%)
  waiting for transfers between devices  39.7 us (21%)
  starting transfers between devices  34.7 us (18%)
  blocking collectives  29.5 us (16%)
  local copies, waits for them, and re-layouts  12.3 us (6%)
    all_to_all x1, blocking collectives, on_device(): slab = lax.all_to_all(slab, 'row', 0, 0, tiled=True)  29.5 us
    ppermute x8, waiting for transfers between devices, swapped(): return lax.ppermute(value, axis, [(i, i ^ bits) for i in range(count)])  19.9 us
    pallas_call x1, Pallas kernels, factor(): pl.pallas_call(factor_kernel, out_shape=shape_of(size, size), in_specs=[v...  18.8 us
    pallas_call x2, Pallas kernels, info_part(): pl.pallas_call(functools.partial(info_kernel, each), out_shape=shape_of(t...  15.6 us
    pallas_call x3, Pallas kernels, pack(): pl.pallas_call(functools.partial(pack_kernel, part * each, each, swapped_...  14 us
    ppermute x8, starting transfers between devices, swapped(): return lax.ppermute(value, axis, [(i, i ^ bits) for i in range(count)])  11.4 us
    all_to_all x2, starting transfers between devices, over(): lax.all_to_all(piece, 'row', 0, 0, axis_index_groups=same_side, tiled=True)  9.42 us
    pallas_call x1, Pallas kernels, prior_part(): pl.pallas_call(functools.partial(prior_kernel, chunk), out_shape=out, gri...  8.77 us
  transfers between devices with their start and end apart: 15, of which 10 were waited for; matrix products, arithmetic and copies ran while one was open for 1% of the time, Pallas kernels for 38%

profile of v1, /device:TPU:0, one launch (start us, length us, event | category | flops | bytes accessed | tf_op | source)
XLA Modules:
  0.0 189.6 jit_solution(11395829800541447916)
XLA Ops:
  0.7 0.9 slice.68
  1.7 5.1 %collective-permute-start.2 = (f32[128,256]{1,0:T(8,128)S(1)}, f32[128,256]{1,0:T(8,128)S(1)}, u32[]{:S(2)}, u32[]{:S(2)}) collective-permute-start(f32[128,256]{1,0:T(8,128)S(1)} %fusion), channel_id=1, source_target_pairs={{0,12},{2,14},{4,8},{6,10},{8,4},{10,6},{12,0},{14,2},{1,13},{3,15... | collective-permute-start | bytes 393224 | tf_op jit(solution)/shard_map/ppermute | solution.py:345
  6.8 0.6 collective-permute-start
  7.4 0.6 stack.63.spot_ref
  8.1 4.3 %pack.4 = f32[4,512,128]{2,1,0:T(8,128)} custom-call(s32[10]{0:T(128)} %stack.63.spot_ref, f32[128,8,8,128]{3,2,1,0:T(8,128)} %bitcast.39), custom_call_target="tpu_custom_call" | custom-call | tf_op jit(solution)/shard_map/pack/pallas_call | solution.py:259
  12.4 5.0 %pack.3 = f32[4,2,512,128]{3,2,1,0:T(8,128)} custom-call(s32[10]{0:T(128)} %stack.63.spot_ref, f32[128,8,8,128]{3,2,1,0:T(8,128)} %bitcast.40, f32[128,8,8,128]{3,2,1,0:T(8,128)} %bitcast.41), custom_call_target="tpu_custom_call" | custom-call | tf_op jit(solution)/shard_map/pack/pallas_call | solution.py:259
  17.3 0.5 collective-permute-done.1
  17.9 4.7 %all-to-all-start = ((f32[4,2,512,128]{3,2,1,0:T(8,128)}), f32[4,2,512,128]{3,2,1,0:T(8,128)S(1)}, u32[]{:S(2)}, u32[]{:S(2)}) async-start(f32[4,2,512,128]{3,2,1,0:T(8,128)} %pack.3), calls=%async_computation | async-start | bytes 4194304 | tf_op jit(solution)/shard_map/all_to_all | solution.py:406
  22.6 1.6 collective-permute-start.4
  24.2 1.5 collective-permute-start.3
  25.7 9.5 %collective-permute-done.4.far_prior = f32[512,256]{1,0:T(8,128)S(1)} collective-permute-done((f32[512,256]{1,0:T(8,128)S(1)}, f32[512,256]{1,0:T(8,128)S(1)}, u32[]{:S(2)}, u32[]{:S(2)}) %collective-permute-start.4) | collective-permute-done | bytes 524320 | tf_op jit(solution)/shard_map/ppermute | solution.py:345
  35.2 2.4 %collective-permute-start.7 = (f32[512,256]{1,0:T(8,128)S(1)}, f32[512,256]{1,0:T(8,128)S(1)}, u32[]{:S(2)}, u32[]{:S(2)}) collective-permute-start(f32[512,256]{1,0:T(8,128)S(1)} %pad_maximum_fusion.1.near_ref), channel_id=1, source_target_pairs={{0,3},{1,2},{2,1},{3,0},{4,7},{5,6},{6,5},{7,4},{8,11},{9,10},{10,... | collective-permute-start | bytes 1572872 | tf_op jit(solution)/shard_map/ppermute | solution.py:368
  37.7 0.5 collective-permute-start.6
  38.2 0.5 collective-permute-start.5
  38.7 8.8 %prior_part.1 = (f32[512,1024]{1,0:T(8,128)}, f32[512,512]{1,0:T(8,128)}) custom-call(s32[10]{0:T(128)} %stack.63.spot_ref, f32[512,256]{1,0:T(8,128)} %bitcast.47, f32[512,256]{1,0:T(8,128)} %copy-done.11, f32[512,8,8,128]{3,2,1,0:T(8,128)} %bitcast.43), custom_call_target="tpu_custom_call" | custom-call | tf_op jit(solution)/shard_map/prior_part/pallas_call | solution.py:169
  47.5 2.8 %collective-permute-done.3.refs_0_ = f32[4,512,128]{2,1,0:T(8,128)S(1)} collective-permute-done((f32[4,512,128]{2,1,0:T(8,128)S(1)}, f32[4,512,128]{2,1,0:T(8,128)S(1)}, u32[]{:S(2)}, u32[]{:S(2)}) %collective-permute-start.3) | collective-permute-done | bytes 1048608 | tf_op jit(solution)/shard_map/ppermute | solution.py:345
  50.3 1.0 copy-done.10
  51.4 4.7 %pack.5 = f32[4,2,512,128]{3,2,1,0:T(8,128)} custom-call(s32[10]{0:T(128)} %stack.63.spot_ref, f32[4,512,128]{2,1,0:T(8,128)} %copy-done.10, f32[128,8,8,128]{3,2,1,0:T(8,128)} %bitcast.42), custom_call_target="tpu_custom_call" | custom-call | tf_op jit(solution)/shard_map/pack/pallas_call | solution.py:259
  56.1 6.2 %collective-permute-done.7.far_next = f32[512,256]{1,0:T(8,128)S(1)} collective-permute-done((f32[512,256]{1,0:T(8,128)S(1)}, f32[512,256]{1,0:T(8,128)S(1)}, u32[]{:S(2)}, u32[]{:S(2)}) %collective-permute-start.7) | collective-permute-done | bytes 524320 | tf_op jit(solution)/shard_map/ppermute | solution.py:368
  62.3 0.8 copy-done.12
  63.1 0.8 copy-done.13
  63.9 6.5 %collective-permute-done.5.near_next = f32[512,256]{1,0:T(8,128)} collective-permute-done((f32[512,256]{1,0:T(8,128)S(1)}, f32[512,256]{1,0:T(8,128)}, u32[]{:S(2)}, u32[]{:S(2)}) %collective-permute-start.5) | collective-permute-done | bytes 524320 | tf_op jit(solution)/shard_map/ppermute | solution.py:345
  70.4 1.4 copy-done.1
  71.8 4.8 %all-to-all-start.2 = ((f32[4,2,512,128]{3,2,1,0:T(8,128)}), f32[4,2,512,128]{3,2,1,0:T(8,128)S(1)}, u32[]{:S(2)}, u32[]{:S(2)}) async-start(f32[4,2,512,128]{3,2,1,0:T(8,128)} %pack.5), calls=%async_computation.2 | async-start | bytes 4194304 | tf_op jit(solution)/shard_map/all_to_all | solution.py:406
  76.5 6.0 %panel_gram.1 = (f32[1024,512]{1,0:T(8,128)}, f32[512,512]{1,0:T(8,128)}) custom-call(s32[10]{0:T(128)} %stack.63.spot_ref, f32[512,256]{1,0:T(8,128)} %copy-done.4, f32[512,256]{1,0:T(8,128)} %collective-permute-done.5.near_next, f32[512,256]{1,0:T(8,128)} %copy-done.13, f32[512,256]{1,0:T(8,128)} %copy-done.12, f32[512,512]{1,0:T(8,128)} %get-tuple-element.62.prior_ref), custom_call_target="tpu_custom_call" | custom-call | tf_op jit(solution)/shard_map/panel_gram/pallas_call | solution.py:213
  82.6 1.5 collective-permute-start.8
  84.2 1.6 collective-permute-start.9
  85.8 0.6 collective-permute-done.8.other_ref
  86.4 1.0 copy-done.6
  87.4 18.8 %factor.1.inverse_ref = f32[512,512]{1,0:T(8,128)} custom-call(f32[512,512]{1,0:T(8,128)} %get-tuple-element.64.own_ref, f32[512,512]{1,0:T(8,128)} %copy-done.6), custom_call_target="tpu_custom_call" | custom-call | tf_op jit(solution)/shard_map/factor/pallas_call | solution.py:133
  106.2 0.5 collective-permute-done.9.far_ref
  106.7 1.0 copy-done.5
  107.7 7.9 %info_part.2.own_ref = f32[512,512]{1,0:T(8,128)} custom-call(s32[10]{0:T(128)} %stack.63.spot_ref, f32[1024,512]{1,0:T(8,128)} %get-tuple-element.70.rows_ref, f32[512,1024]{1,0:T(8,128)} %get-tuple-element.67.prior_ref, f32[4,512,128]{2,1,0:T(8,128)} %copy-done.5, f32[4,2,512,128]{3,2,1,0:T(8,128)} %copy-done.1), custom_call_target="tpu_custom_call" | custom-call | tf_op jit(solution)/shard_map/info_part/pallas_call | solution.py:292
  115.7 1.8 collective-permute-start.10
  117.5 2.4 %collective-permute-done.10.other_ref = f32[512,512]{1,0:T(8,128)S(1)} collective-permute-done((f32[512,512]{1,0:T(8,128)}, f32[512,512]{1,0:T(8,128)S(1)}, u32[]{:S(2)}, u32[]{:S(2)}) %collective-permute-start.10) | collective-permute-done | bytes 1048608 | tf_op jit(solution)/shard_map/ppermute | solution.py:349
  119.9 1.0 copy-done.8
  120.9 4.4 %slab_part.2 = f32[8,256,128]{2,1,0:T(8,128)} custom-call(s32[10]{0:T(128)} %stack.63.spot_ref, f32[512,512]{1,0:T(8,128)} %factor.1.inverse_ref, f32[512,512]{1,0:T(8,128)} %info_part.2.own_ref, f32[512,512]{1,0:T(8,128)} %copy-done.8), custom_call_target="tpu_custom_call" | custom-call | tf_op jit(solution)/shard_map/slab_part/pallas_call | solution.py:333
  125.3 6.0 %all-to-all-start.1 = ((f32[8,256,128]{2,1,0:T(8,128)}), f32[8,256,128]{2,1,0:T(8,128)S(1)}, u32[]{:S(2)}, u32[]{:S(2)}) async-start(f32[8,256,128]{2,1,0:T(8,128)} %slab_part.2), calls=%async_computation.1 | async-start | bytes 2097152 | tf_op jit(solution)/shard_map/all_to_all | solution.py:443
  131.3 0.7 stack.70.spot_ref
  132.0 7.6 %info_part.3.own_ref = f32[512,512]{1,0:T(8,128)} custom-call(s32[10]{0:T(128)} %stack.70.spot_ref, f32[1024,512]{1,0:T(8,128)} %get-tuple-element.70.rows_ref, f32[512,1024]{1,0:T(8,128)} %get-tuple-element.67.prior_ref, f32[4,2,512,128]{3,2,1,0:T(8,128)} %copy-done, f32[4,2,512,128]{3,2,1,0:T(8,128)} %copy-done), custom_call_target="tpu_custom_call" | custom-call | tf_op jit(solution)/shard_map/info_part/pallas_call | solution.py:292
  139.7 2.0 %collective-permute-start.11 = (f32[512,512]{1,0:T(8,128)}, f32[512,512]{1,0:T(8,128)S(1)}, u32[]{:S(2)}, u32[]{:S(2)}) collective-permute-start(f32[512,512]{1,0:T(8,128)} %info_part.3.own_ref), channel_id=1, source_target_pairs={{0,16},{1,17},{2,18},{3,19},{4,20},{5,21},{6,22},{7,23},{8,24},{9,... | collective-permute-start | bytes 3145736 | tf_op jit(solution)/shard_map/ppermute | solution.py:349
  141.7 2.4 %collective-permute-done.11.other_ref = f32[512,512]{1,0:T(8,128)S(1)} collective-permute-done((f32[512,512]{1,0:T(8,128)}, f32[512,512]{1,0:T(8,128)S(1)}, u32[]{:S(2)}, u32[]{:S(2)}) %collective-permute-start.11) | collective-permute-done | bytes 1048608 | tf_op jit(solution)/shard_map/ppermute | solution.py:349
  144.1 1.0 copy-done.7
  145.1 4.3 %slab_part.3 = f32[8,256,128]{2,1,0:T(8,128)} custom-call(s32[10]{0:T(128)} %stack.70.spot_ref, f32[512,512]{1,0:T(8,128)} %factor.1.inverse_ref, f32[512,512]{1,0:T(8,128)} %info_part.3.own_ref, f32[512,512]{1,0:T(8,128)} %copy-done.7), custom_call_target="tpu_custom_call" | custom-call | tf_op jit(solution)/shard_map/slab_part/pallas_call | solution.py:333
  149.4 8.2 %all-to-all-done.1 = f32[8,256,128]{2,1,0:T(8,128)S(1)} async-done(((f32[8,256,128]{2,1,0:T(8,128)}), f32[8,256,128]{2,1,0:T(8,128)S(1)}, u32[]{:S(2)}, u32[]{:S(2)}) %all-to-all-start.1) | async-done | bytes 1048608 | tf_op jit(solution)/shard_map/all_to_all | solution.py:443
  157.6 29.5 %all_to_all.20 = f32[8,256,128]{2,1,0:T(8,128)S(1)} all-to-all(f32[8,256,128]{2,1,0:T(8,128)} %slab_part.3), channel_id=1, replica_groups=mesh['section'=2,'row'=8,'col'=2] {'row'}, dimensions={0} | all-to-all | bytes 2097152 | tf_op jit(solution)/shard_map/all_to_all | solution.py:443
  187.2 0.5 pad_maximum_fusion
  187.7 1.9 %copy.6 = f32[64,8,2,4,128]{4,3,2,1,0:T(4,128)} copy(f32[64,8,2,4,128]{4,3,0,1,2:T(4,128)S(1)} %pad_maximum_fusion) | data formatting | bytes 4194304 | tf_op jit(solution)/shard_map/scatter | solution.py:445
  (33 shorter events, 0.3 us)
Async XLA Ops:
  1.7 15.7 %collective-permute-start.2 = (f32[128,256]{1,0:T(8,128)S(1)}, f32[128,256]{1,0:T(8,128)S(1)}, u32[]{:S(2)}, u32[]{:S(2)}) collective-permute-start(f32[128,256]{1,0:T(8,128)S(1)} %fusion), channel_id=1, source_target_pairs={{0,12},{2,14},{4,8},{6,10},{8,4},{10,6},{12,0},{14,2},{1,13},{3,15... | collective-permute-start | bytes 393224 | tf_op jit(solution)/shard_map/ppermute | solution.py:345
  6.8 11.1 %collective-permute-start.1 = (f32[128,256]{1,0:T(8,128)S(1)}, f32[128,256]{1,0:T(8,128)S(1)}, u32[]{:S(2)}, u32[]{:S(2)}) collective-permute-start(f32[128,256]{1,0:T(8,128)S(1)} %fusion), channel_id=1, source_target_pairs={{0,8},{2,10},{4,12},{6,14},{8,0},{10,2},{12,4},{14,6},{1,9},{3,11}... | collective-permute-start | bytes 393224 | tf_op jit(solution)/shard_map/ppermute | solution.py:345
  6.8 11.1 %collective-permute-start = (f32[128,256]{1,0:T(8,128)S(1)}, f32[128,256]{1,0:T(8,128)S(1)}, u32[]{:S(2)}, u32[]{:S(2)}) collective-permute-start(f32[128,256]{1,0:T(8,128)S(1)} %fusion), channel_id=1, source_target_pairs={{0,4},{2,6},{4,0},{6,2},{8,12},{10,14},{12,8},{14,10},{1,5},{3,7},... | collective-permute-start | bytes 393224 | tf_op jit(solution)/shard_map/ppermute | solution.py:345
  17.9 20.3 %copy-start.4 = (f32[512,256]{1,0:T(8,128)}, f32[512,256]{1,0:T(8,128)S(1)}, u32[]{:S(2)}) copy-start(f32[512,256]{1,0:T(8,128)S(1)} %pad_maximum_fusion.1.near_ref) | copy-start | bytes 1572868
  17.9 4.7 %slice-start = ((f32[512,32,1,256]{3,2,1,0:T(1,128)}), f32[512,1,1,256]{3,2,1,0:T(1,128)S(1)}, s32[]{:S(2)}) async-start(f32[512,32,1,256]{3,2,1,0:T(1,128)} %param.7), calls=%async_computation.4 | async-start | bytes 1048576 | tf_op jit(solution)/shard_map/slice | solution.py:409
  17.9 52.5 %all-to-all-start = ((f32[4,2,512,128]{3,2,1,0:T(8,128)}), f32[4,2,512,128]{3,2,1,0:T(8,128)S(1)}, u32[]{:S(2)}, u32[]{:S(2)}) async-start(f32[4,2,512,128]{3,2,1,0:T(8,128)} %pack.3), calls=%async_computation | async-start | bytes 4194304 | tf_op jit(solution)/shard_map/all_to_all | solution.py:406
  22.6 1.6 copy-start.9
  22.6 16.1 %copy-start.3 = (f32[512,1,1,256]{3,0,2,1:T(8,128)}, f32[512,1,1,256]{3,0,2,1:T(8,128)S(1)}, u32[]{:S(2)}) copy-start(f32[512,1,1,256]{3,0,2,1:T(8,128)S(1)} %copy.13) | copy-start | bytes 1572868
  22.6 12.6 %collective-permute-start.4 = (f32[512,256]{1,0:T(8,128)S(1)}, f32[512,256]{1,0:T(8,128)S(1)}, u32[]{:S(2)}, u32[]{:S(2)}) collective-permute-start(f32[512,256]{1,0:T(8,128)S(1)} %bitcast.46), channel_id=1, source_target_pairs={{0,1},{1,0},{2,3},{3,2},{4,5},{5,4},{6,7},{7,6},{8,9},{9,8},{10,11... | collective-permute-start | bytes 1572872 | tf_op jit(solution)/shard_map/ppermute | solution.py:345
  24.2 26.1 %collective-permute-start.3 = (f32[4,512,128]{2,1,0:T(8,128)S(1)}, f32[4,512,128]{2,1,0:T(8,128)S(1)}, u32[]{:S(2)}, u32[]{:S(2)}) collective-permute-start(f32[4,512,128]{2,1,0:T(8,128)S(1)} %copy-done.9), channel_id=1, source_target_pairs={{0,2},{2,0},{4,6},{6,4},{8,10},{10,8},{12,14},{14,12},{1,3},{3,1},... | collective-permute-start | bytes 3145736 | tf_op jit(solution)/shard_map/ppermute | solution.py:345
  35.2 3.5 %copy-start.11 = (f32[512,256]{1,0:T(8,128)}, f32[512,256]{1,0:T(8,128)S(1)}, u32[]{:S(2)}) copy-start(f32[512,256]{1,0:T(8,128)S(1)} %collective-permute-done.4.far_prior) | copy-start | bytes 1572868
  35.2 27.1 %collective-permute-start.7 = (f32[512,256]{1,0:T(8,128)S(1)}, f32[512,256]{1,0:T(8,128)S(1)}, u32[]{:S(2)}, u32[]{:S(2)}) collective-permute-start(f32[512,256]{1,0:T(8,128)S(1)} %pad_maximum_fusion.1.near_ref), channel_id=1, source_target_pairs={{0,3},{1,2},{2,1},{3,0},{4,7},{5,6},{6,5},{7,4},{8,11},{9,10},{10,... | collective-permute-start | bytes 1572872 | tf_op jit(solution)/shard_map/ppermute | solution.py:368
  37.7 24.6 %collective-permute-start.6 = (f32[512,256]{1,0:T(8,128)S(1)}, f32[512,256]{1,0:T(8,128)S(1)}, u32[]{:S(2)}, u32[]{:S(2)}) collective-permute-start(f32[512,256]{1,0:T(8,128)S(1)} %pad_maximum_fusion.1.near_ref), channel_id=1, source_target_pairs={{0,1},{1,0},{2,3},{3,2},{4,5},{5,4},{6,7},{7,6},{8,9},{9,8},{10,11... | collective-permute-start | bytes 1572872 | tf_op jit(solution)/shard_map/ppermute | solution.py:345
  38.2 32.2 %collective-permute-start.5 = (f32[512,256]{1,0:T(8,128)S(1)}, f32[512,256]{1,0:T(8,128)}, u32[]{:S(2)}, u32[]{:S(2)}) collective-permute-start(f32[512,256]{1,0:T(8,128)S(1)} %pad_maximum_fusion.1.near_ref), channel_id=1, source_target_pairs={{0,2},{2,0},{4,6},{6,4},{8,10},{10,8},{12,14},{14,12},{1,3},{3,1},... | collective-permute-start | bytes 1572872 | tf_op jit(solution)/shard_map/ppermute | solution.py:345
  50.3 1.0 copy-start.10
  62.3 0.8 copy-start.12
  63.1 0.8 copy-start.13
  70.4 1.4 copy-start.1
  71.8 53.5 %all-to-all-start.2 = ((f32[4,2,512,128]{3,2,1,0:T(8,128)}), f32[4,2,512,128]{3,2,1,0:T(8,128)S(1)}, u32[]{:S(2)}, u32[]{:S(2)}) async-start(f32[4,2,512,128]{3,2,1,0:T(8,128)} %pack.5), calls=%async_computation.2 | async-start | bytes 4194304 | tf_op jit(solution)/shard_map/all_to_all | solution.py:406
  76.5 7.6 %copy-start.2 = (f32[4,2,512,128]{3,2,1,0:T(8,128)S(1)}, f32[4,2,512,128]{3,2,1,0:T(8,128)}, u32[]{:S(2)}) copy-start(f32[4,2,512,128]{3,2,1,0:T(8,128)} %copy-done.1) | copy-start | bytes 6291460
  82.6 3.8 %collective-permute-start.8 = (f32[512,512]{1,0:T(8,128)}, f32[512,512]{1,0:T(8,128)S(1)}, u32[]{:S(2)}, u32[]{:S(2)}) collective-permute-start(f32[512,512]{1,0:T(8,128)} %get-tuple-element.64.own_ref), channel_id=1, source_target_pairs={{0,16},{1,17},{2,18},{3,19},{4,20},{5,21},{6,22},{7,23},{8,24},{9,... | collective-permute-start | bytes 3145736 | tf_op jit(solution)/shard_map/ppermute | solution.py:349
  84.2 22.5 %collective-permute-start.9 = (f32[4,512,128]{2,1,0:T(8,128)S(1)}, f32[4,512,128]{2,1,0:T(8,128)S(1)}, u32[]{:S(2)}, u32[]{:S(2)}) collective-permute-start(f32[4,512,128]{2,1,0:T(8,128)S(1)} %slice_bitcast_fusion), channel_id=1, source_target_pairs={{0,2},{2,0},{4,6},{6,4},{8,10},{10,8},{12,14},{14,12},{1,3},{3,1},... | collective-permute-start | bytes 3145736 | tf_op jit(solution)/shard_map/ppermute | solution.py:345
  86.4 1.0 copy-start.6
  106.7 1.0 copy-start.5
  115.7 4.2 %collective-permute-start.10 = (f32[512,512]{1,0:T(8,128)}, f32[512,512]{1,0:T(8,128)S(1)}, u32[]{:S(2)}, u32[]{:S(2)}) collective-permute-start(f32[512,512]{1,0:T(8,128)} %info_part.2.own_ref), channel_id=1, source_target_pairs={{0,16},{1,17},{2,18},{3,19},{4,20},{5,21},{6,22},{7,23},{8,24},{9,... | collective-permute-start | bytes 3145736 | tf_op jit(solution)/shard_map/ppermute | solution.py:349
  119.9 1.0 copy-start.8
  125.3 6.7 %copy-start = (f32[4,2,512,128]{3,2,1,0:T(8,128)}, f32[4,2,512,128]{3,2,1,0:T(8,128)S(1)}, u32[]{:S(2)}) copy-start(f32[4,2,512,128]{3,2,1,0:T(8,128)S(1)} %all-to-all-done.2.far_ref.near_ref) | copy-start | bytes 6291460
  125.3 32.3 %all-to-all-start.1 = ((f32[8,256,128]{2,1,0:T(8,128)}), f32[8,256,128]{2,1,0:T(8,128)S(1)}, u32[]{:S(2)}, u32[]{:S(2)}) async-start(f32[8,256,128]{2,1,0:T(8,128)} %slab_part.2), calls=%async_computation.1 | async-start | bytes 2097152 | tf_op jit(solution)/shard_map/all_to_all | solution.py:443
  139.7 4.5 %collective-permute-start.11 = (f32[512,512]{1,0:T(8,128)}, f32[512,512]{1,0:T(8,128)S(1)}, u32[]{:S(2)}, u32[]{:S(2)}) collective-permute-start(f32[512,512]{1,0:T(8,128)} %info_part.3.own_ref), channel_id=1, source_target_pairs={{0,16},{1,17},{2,18},{3,19},{4,20},{5,21},{6,22},{7,23},{8,24},{9,... | collective-permute-start | bytes 3145736 | tf_op jit(solution)/shard_map/ppermute | solution.py:349
  144.1 1.0 copy-start.7

commit v2 on v1

--- a/solution.py
+++ b/solution.py
@@ -340,6 +340,40 @@
     )(spot, inverse, own, other)
 
 
+def sides_kernel(count, spot_ref, inverse_ref, own_ref, other_ref, near_ref, far_ref, work):
+    total, width = own_ref.shape
+    own_rows, chunk = total // count, width // LANES
+    half = total // 2
+    tile = (own_rows, LANES)
+    row_ids = lax.broadcasted_iota(jnp.int32, tile, 0)
+    lane_ids = lax.broadcasted_iota(jnp.int32, tile, 1)
+    info = own_ref[...] + other_ref[...]
+    for lower in range(2):
+        depth = (lower + 1) * half
+        work[lower * half : depth, :] = dot(inverse_ref[lower * half : depth, :depth], info[:depth, :], 1, 0)
+    for change, out_ref in enumerate((near_ref, far_ref)):
+        for pair in range(count // 2):
+            first = pl.multiple_of((2 * pair + (spot_ref[2] + change) % 2) * own_rows, own_rows)
+            for b in range(chunk):
+                part = work[pl.ds(first, own_rows), b * LANES : (b + 1) * LANES]
+                kept = jnp.where(spot_ref[SPOTS + b] + lane_ids >= row_ids + first, part, 0.0)
+                out_ref[pair, pl.ds(b, own_rows, stride=chunk), :] = kept
+
+
+def slab_sides(count, spot, inverse, own, other):
+    total, width = own.shape
+    out = shape_of(count // 2, total // count * width // LANES, LANES)
+    return pl.pallas_call(
+        functools.partial(sides_kernel, count),
+        out_shape=(out, out),
+        in_specs=[pl.BlockSpec(memory_space=pltpu.SMEM)] + [vmem_spec()] * 3,
+        out_specs=(vmem_spec(),) * 2,
+        scratch_shapes=[pltpu.VMEM((total, width), jnp.float32)],
+        compiler_params=params(),
+        name="slab_sides",
+    )(spot, inverse, own, other)
+
+
 def swapped(value, axis, bits):
     count = lax.axis_size(axis)
     return lax.ppermute(value, axis, [(i, i ^ bits) for i in range(count)])
@@ -439,10 +473,26 @@
             rows_panel, other = lax.optimization_barrier((rows_panel, other))
         info = info_part(part, each, spots[part], rows_panel, prior_info, far, near)
         other = handed_on(info)
-        slab = slab_part(rows, spots[part], inverse, info, other)
-        slab = lax.all_to_all(slab, "row", 0, 0, tiled=True)
-        slab = slab.reshape(rows, total // rows, each, LANES).transpose(1, 0, 2, 3)
-        out = out.at[:, :, part].set(slab)
+        if part == 0:
+            slab = slab_part(rows, spots[part], inverse, info, other)
+            slab = lax.all_to_all(slab, "row", 0, 0, tiled=True)
+            continue
+        sides = list(slab_sides(rows, spots[part], inverse, info, other))
+        sides[1] = swapped(sides[1], "row", 1)
+        placed = []
+        for change, side in enumerate(sides):
+            for k in range(rows // 2):
+                piece = lax.dynamic_index_in_dim(side, (row // 2) ^ k, 0, keepdims=False)
+                piece = swapped(piece, "row", 2 * k) if k else piece
+                placed.append((row ^ (2 * k + change), piece.reshape(total // rows, each, LANES)))
+        slab, received = lax.optimization_barrier((slab, [piece for _, piece in placed]))
+        placed = [(source, piece) for (source, _), piece in zip(placed, received)]
+    slab = slab.reshape(rows, total // rows, each, LANES).transpose(1, 0, 2, 3)
+    out = out.at[:, :, 0].set(slab)
+    if parts > 1:
+        out = out.reshape(total // rows, rows * parts, each, LANES)
+        for source, piece in placed:
+            out = lax.dynamic_update_index_in_dim(out, piece, source * parts + 1, 1)
     out = out.reshape(total // rows, rows * chunk, LANES)[:, :blocks]
     return out.reshape(1, total // rows, cycles, 1, width)
 

time: 190 us -> 185 us (0.974)
  blocking collectives: 29.5 us -> 0 us
  starting transfers between devices: 34.7 us -> 46.1 us
  waiting for transfers between devices: 39.7 us -> 50.7 us
  local copies, waits for them, and re-layouts: 12.3 us -> 14.6 us
    all_to_all x1 -> x0, blocking collectives: 29.5 us -> none  [on_device(): slab = lax.all_to_all(slab, 'row', 0, 0, tiled=True)]
    ppermute x8 -> x15, waiting for transfers between devices: 19.9 us -> 37.1 us  [swapped(): return lax.ppermute(value, axis, [(i, i ^ bits) for i in range(count)])]
    ppermute x8 -> x15, starting transfers between devices: 11.4 us -> 24.4 us  [swapped(): return lax.ppermute(value, axis, [(i, i ^ bits) for i in range(count)])]
    all_to_all x1, waiting for transfers between devices: 8.21 us -> 0.01 us  [on_device(): slab = lax.all_to_all(slab, 'row', 0, 0, tiled=True)]
    pallas_call x0 -> x1, Pallas kernels: none -> 4.48 us  [slab_sides(): pl.pallas_call(functools.partial(sides_kernel, count), out_shape=(out, ou...]
    pallas_call x2 -> x1, Pallas kernels: 8.74 us -> 4.36 us  [slab_part(): pl.pallas_call(functools.partial(slab_kernel, count), out_shape=shape_of(...]
    dynamic_update_slice x0 -> x9, local copies, waits for them, and re-layouts: none -> 2.82 us  [on_device(): out = lax.dynamic_update_index_in_dim(out, piece, source * parts + 1, 1)]
    ppermute x1, starting transfers between devices: 2.45 us -> 0.48 us  [all_panels(): far = [swapped(near, 'col', 1), lax.ppermute(near, ('row', 'col'), order)]]
  transfers between devices with their start and end apart: 15 -> 22, of which waited for: 10 -> 12; matrix products, arithmetic and copies ran while one was open for 1% -> 1% of each run, Pallas kernels for 38% -> 39%
where the time goes in v2:
time: 185 us; the launch traced here: 184 us
  Pallas kernels  72 us (39%)
  waiting for transfers between devices  50.7 us (27%)
  starting transfers between devices  46.1 us (25%)
  local copies, waits for them, and re-layouts  14.6 us (8%)
    ppermute x15, waiting for transfers between devices, swapped(): return lax.ppermute(value, axis, [(i, i ^ bits) for i in range(count)])  37.1 us
    ppermute x15, starting transfers between devices, swapped(): return lax.ppermute(value, axis, [(i, i ^ bits) for i in range(count)])  24.4 us
    pallas_call x1, Pallas kernels, factor(): pl.pallas_call(factor_kernel, out_shape=shape_of(size, size), in_specs=[v...  18.8 us
    pallas_call x2, Pallas kernels, info_part(): pl.pallas_call(functools.partial(info_kernel, each), out_shape=shape_of(t...  15.5 us
    pallas_call x3, Pallas kernels, pack(): pl.pallas_call(functools.partial(pack_kernel, part * each, each, swapped_...  14 us
    all_to_all x2, starting transfers between devices, over(): lax.all_to_all(piece, 'row', 0, 0, axis_index_groups=same_side, tiled=True)  9.68 us
    pallas_call x1, Pallas kernels, prior_part(): pl.pallas_call(functools.partial(prior_kernel, chunk), out_shape=out, gri...  8.77 us
    ppermute x1, waiting for transfers between devices, all_panels(): far = [swapped(near, 'col', 1), lax.ppermute(near, ('row', 'col'), order)]  8.14 us
  transfers between devices with their start and end apart: 22, of which 12 were waited for; matrix products, arithmetic and copies ran while one was open for 1% of the time, Pallas kernels for 39%

profile of v2, /device:TPU:0, one launch (start us, length us, event | category | flops | bytes accessed | tf_op | source)
XLA Modules:
  0.0 184.4 jit_solution(6701135830192884965)
XLA Ops:
  0.0 0.9 slice.38
  1.7 3.1 %collective-permute-start = (f32[128,256]{1,0:T(8,128)S(1)}, f32[128,256]{1,0:T(8,128)S(1)}, u32[]{:S(2)}, u32[]{:S(2)}) collective-permute-start(f32[128,256]{1,0:T(8,128)S(1)} %fusion), channel_id=1, source_target_pairs={{0,4},{2,6},{4,0},{6,2},{8,12},{10,14},{12,8},{14,10},{1,5},{3,7},... | collective-permute-start | bytes 393224 | tf_op jit(solution)/shard_map/ppermute | solution.py:379
  4.8 2.6 %collective-permute-start.1 = (f32[128,256]{1,0:T(8,128)S(1)}, f32[128,256]{1,0:T(8,128)S(1)}, u32[]{:S(2)}, u32[]{:S(2)}) collective-permute-start(f32[128,256]{1,0:T(8,128)S(1)} %fusion), channel_id=1, source_target_pairs={{0,8},{2,10},{4,12},{6,14},{8,0},{10,2},{12,4},{14,6},{1,9},{3,11}... | collective-permute-start | bytes 393224 | tf_op jit(solution)/shard_map/ppermute | solution.py:379
  8.0 5.0 %pack.3 = f32[4,2,512,128]{3,2,1,0:T(8,128)} custom-call(s32[10]{0:T(128)} %stack.63.spot_ref, f32[128,8,8,128]{3,2,1,0:T(8,128)} %bitcast.64, f32[128,8,8,128]{3,2,1,0:T(8,128)} %bitcast.65), custom_call_target="tpu_custom_call" | custom-call | tf_op jit(solution)/shard_map/pack/pallas_call | solution.py:259
  13.0 4.3 %pack.4 = f32[4,512,128]{2,1,0:T(8,128)} custom-call(s32[10]{0:T(128)} %stack.63.spot_ref, f32[128,8,8,128]{3,2,1,0:T(8,128)} %bitcast.66), custom_call_target="tpu_custom_call" | custom-call | tf_op jit(solution)/shard_map/pack/pallas_call | solution.py:259
  17.8 4.9 %all-to-all-start = ((f32[4,2,512,128]{3,2,1,0:T(8,128)}), f32[4,2,512,128]{3,2,1,0:T(8,128)S(1)}, u32[]{:S(2)}, u32[]{:S(2)}) async-start(f32[4,2,512,128]{3,2,1,0:T(8,128)} %pack.3), calls=%async_computation | async-start | bytes 4194304 | tf_op jit(solution)/shard_map/all_to_all | solution.py:440
  22.7 1.6 collective-permute-start.4
  24.3 1.5 collective-permute-start.3
  25.8 9.5 %collective-permute-done.4.far_prior = f32[512,256]{1,0:T(8,128)S(1)} collective-permute-done((f32[512,256]{1,0:T(8,128)S(1)}, f32[512,256]{1,0:T(8,128)S(1)}, u32[]{:S(2)}, u32[]{:S(2)}) %collective-permute-start.4) | collective-permute-done | bytes 524320 | tf_op jit(solution)/shard_map/ppermute | solution.py:379
  35.3 1.5 collective-permute-start.5
  36.8 1.5 collective-permute-start.6
  38.8 8.8 %prior_part.1 = (f32[512,1024]{1,0:T(8,128)}, f32[512,512]{1,0:T(8,128)}) custom-call(s32[10]{0:T(128)} %stack.63.spot_ref, f32[512,256]{1,0:T(8,128)} %bitcast.73, f32[512,256]{1,0:T(8,128)} %copy-done.11, f32[512,8,8,128]{3,2,1,0:T(8,128)} %bitcast.68), custom_call_target="tpu_custom_call" | custom-call | tf_op jit(solution)/shard_map/prior_part/pallas_call | solution.py:169
  47.6 2.8 %collective-permute-done.3.refs_0_ = f32[4,512,128]{2,1,0:T(8,128)S(1)} collective-permute-done((f32[4,512,128]{2,1,0:T(8,128)S(1)}, f32[4,512,128]{2,1,0:T(8,128)S(1)}, u32[]{:S(2)}, u32[]{:S(2)}) %collective-permute-start.3) | collective-permute-done | bytes 1048608 | tf_op jit(solution)/shard_map/ppermute | solution.py:379
  50.4 1.0 copy-done.10
  51.4 4.7 %pack.5 = f32[4,2,512,128]{3,2,1,0:T(8,128)} custom-call(s32[10]{0:T(128)} %stack.63.spot_ref, f32[4,512,128]{2,1,0:T(8,128)} %copy-done.10, f32[128,8,8,128]{3,2,1,0:T(8,128)} %bitcast.67), custom_call_target="tpu_custom_call" | custom-call | tf_op jit(solution)/shard_map/pack/pallas_call | solution.py:259
  56.1 5.5 %collective-permute-done.5.near_next = f32[512,256]{1,0:T(8,128)S(1)} collective-permute-done((f32[512,256]{1,0:T(8,128)S(1)}, f32[512,256]{1,0:T(8,128)S(1)}, u32[]{:S(2)}, u32[]{:S(2)}) %collective-permute-start.5) | collective-permute-done | bytes 524320 | tf_op jit(solution)/shard_map/ppermute | solution.py:379
  61.6 0.8 copy-done.12
  62.4 0.8 copy-done.13
  63.2 8.1 %collective-permute-done.7.far_next = f32[512,256]{1,0:T(8,128)} collective-permute-done((f32[512,256]{1,0:T(8,128)S(1)}, f32[512,256]{1,0:T(8,128)}, u32[]{:S(2)}, u32[]{:S(2)}) %collective-permute-start.7) | collective-permute-done | bytes 524320 | tf_op jit(solution)/shard_map/ppermute | solution.py:402
  71.4 1.4 copy-done.1
  72.7 4.8 %all-to-all-start.2 = ((f32[4,2,512,128]{3,2,1,0:T(8,128)}), f32[4,2,512,128]{3,2,1,0:T(8,128)S(1)}, u32[]{:S(2)}, u32[]{:S(2)}) async-start(f32[4,2,512,128]{3,2,1,0:T(8,128)} %pack.5), calls=%async_computation.2 | async-start | bytes 4194304 | tf_op jit(solution)/shard_map/all_to_all | solution.py:440
  77.5 6.0 %panel_gram.1 = (f32[1024,512]{1,0:T(8,128)}, f32[512,512]{1,0:T(8,128)}) custom-call(s32[10]{0:T(128)} %stack.63.spot_ref, f32[512,256]{1,0:T(8,128)} %copy-done.4, f32[512,256]{1,0:T(8,128)} %copy-done.12, f32[512,256]{1,0:T(8,128)} %copy-done.13, f32[512,256]{1,0:T(8,128)} %collective-permute-done.7.far_next, f32[512,512]{1,0:T(8,128)} %get-tuple-element.61.prior_ref), custom_call_target="tpu_custom_call" | custom-call | tf_op jit(solution)/shard_map/panel_gram/pallas_call | solution.py:213
  83.6 1.5 collective-permute-start.8
  85.2 1.6 collective-permute-start.9
  87.3 1.0 copy-done.6
  88.3 18.8 %factor.1.inverse_ref = f32[512,512]{1,0:T(8,128)} custom-call(f32[512,512]{1,0:T(8,128)} %get-tuple-element.63.own_ref, f32[512,512]{1,0:T(8,128)} %copy-done.6), custom_call_target="tpu_custom_call" | custom-call | tf_op jit(solution)/shard_map/factor/pallas_call | solution.py:133
  107.5 1.0 copy-done.5
  108.5 7.9 %info_part.2.own_ref = f32[512,512]{1,0:T(8,128)} custom-call(s32[10]{0:T(128)} %stack.63.spot_ref, f32[1024,512]{1,0:T(8,128)} %get-tuple-element.69.rows_ref, f32[512,1024]{1,0:T(8,128)} %get-tuple-element.66.prior_ref, f32[4,512,128]{2,1,0:T(8,128)} %copy-done.5, f32[4,2,512,128]{3,2,1,0:T(8,128)} %copy-done.1), custom_call_target="tpu_custom_call" | custom-call | tf_op jit(solution)/shard_map/info_part/pallas_call | solution.py:292
  116.4 2.0 %collective-permute-start.10 = (f32[512,512]{1,0:T(8,128)}, f32[512,512]{1,0:T(8,128)S(1)}, u32[]{:S(2)}, u32[]{:S(2)}) collective-permute-start(f32[512,512]{1,0:T(8,128)} %info_part.2.own_ref), channel_id=1, source_target_pairs={{0,16},{1,17},{2,18},{3,19},{4,20},{5,21},{6,22},{7,23},{8,24},{9,... | collective-permute-start | bytes 3145736 | tf_op jit(solution)/shard_map/ppermute | solution.py:383
  118.4 2.4 %collective-permute-done.10.other_ref = f32[512,512]{1,0:T(8,128)S(1)} collective-permute-done((f32[512,512]{1,0:T(8,128)}, f32[512,512]{1,0:T(8,128)S(1)}, u32[]{:S(2)}, u32[]{:S(2)}) %collective-permute-start.10) | collective-permute-done | bytes 1048608 | tf_op jit(solution)/shard_map/ppermute | solution.py:383
  120.8 1.0 copy-done.7
  121.8 4.4 %slab_part.1 = f32[8,256,128]{2,1,0:T(8,128)} custom-call(s32[10]{0:T(128)} %stack.63.spot_ref, f32[512,512]{1,0:T(8,128)} %factor.1.inverse_ref, f32[512,512]{1,0:T(8,128)} %info_part.2.own_ref, f32[512,512]{1,0:T(8,128)} %copy-done.7), custom_call_target="tpu_custom_call" | custom-call | tf_op jit(solution)/shard_map/slab_part/pallas_call | solution.py:333
  126.1 6.0 %all-to-all-start.1 = ((f32[8,256,128]{2,1,0:T(8,128)}), f32[8,256,128]{2,1,0:T(8,128)S(1)}, u32[]{:S(2)}, u32[]{:S(2)}) async-start(f32[8,256,128]{2,1,0:T(8,128)} %slab_part.1), calls=%async_computation.1 | async-start | bytes 2097152 | tf_op jit(solution)/shard_map/all_to_all | solution.py:478
  132.8 7.6 %info_part.3.own_ref = f32[512,512]{1,0:T(8,128)} custom-call(s32[10]{0:T(128)} %stack.70.spot_ref, f32[1024,512]{1,0:T(8,128)} %get-tuple-element.69.rows_ref, f32[512,1024]{1,0:T(8,128)} %get-tuple-element.66.prior_ref, f32[4,2,512,128]{3,2,1,0:T(8,128)} %copy-done, f32[4,2,512,128]{3,2,1,0:T(8,128)} %copy-done), custom_call_target="tpu_custom_call" | custom-call | tf_op jit(solution)/shard_map/info_part/pallas_call | solution.py:292
  140.4 2.0 %collective-permute-start.11 = (f32[512,512]{1,0:T(8,128)}, f32[512,512]{1,0:T(8,128)S(1)}, u32[]{:S(2)}, u32[]{:S(2)}) collective-permute-start(f32[512,512]{1,0:T(8,128)} %info_part.3.own_ref), channel_id=1, source_target_pairs={{0,16},{1,17},{2,18},{3,19},{4,20},{5,21},{6,22},{7,23},{8,24},{9,... | collective-permute-start | bytes 3145736 | tf_op jit(solution)/shard_map/ppermute | solution.py:383
  142.5 2.4 %collective-permute-done.11.other_ref = f32[512,512]{1,0:T(8,128)S(1)} collective-permute-done((f32[512,512]{1,0:T(8,128)}, f32[512,512]{1,0:T(8,128)S(1)}, u32[]{:S(2)}, u32[]{:S(2)}) %collective-permute-start.11) | collective-permute-done | bytes 1048608 | tf_op jit(solution)/shard_map/ppermute | solution.py:383
  144.9 1.0 copy-done.8
  145.9 4.5 %slab_sides.1 = (f32[4,256,128]{2,1,0:T(8,128)}, f32[4,256,128]{2,1,0:T(8,128)}) custom-call(s32[10]{0:T(128)} %stack.70.spot_ref, f32[512,512]{1,0:T(8,128)} %factor.1.inverse_ref, f32[512,512]{1,0:T(8,128)} %info_part.3.own_ref, f32[512,512]{1,0:T(8,128)} %copy-done.8), custom_call_target="tpu_custom_call" | custom-call | tf_op jit(solution)/shard_map/slab_sides/pallas_call | solution.py:366
  150.3 1.8 collective-permute-start.15
  152.1 1.1 dynamic-slice_bitcast_fusion.3
  153.2 1.5 collective-permute-start.12
  154.8 2.4 %collective-permute-start.13 = (f32[256,128]{1,0:T(8,128)S(1)}, f32[256,128]{1,0:T(8,128)S(1)}, u32[]{:S(2)}, u32[]{:S(2)}) collective-permute-start(f32[256,128]{1,0:T(8,128)S(1)} %get-tuple-element.88), channel_id=1, source_target_pairs={{0,8},{2,10},{4,12},{6,14},{8,0},{10,2},{12,4},{14,6},{1,9},{3,11}... | collective-permute-start | bytes 393224 | tf_op jit(solution)/shard_map/ppermute | solution.py:379
  157.7 8.2 %collective-permute-done.15 = f32[4,256,128]{2,1,0:T(8,128)S(1)} collective-permute-done((f32[4,256,128]{2,1,0:T(8,128)}, f32[4,256,128]{2,1,0:T(8,128)S(1)}, u32[]{:S(2)}, u32[]{:S(2)}) %collective-permute-start.15) | collective-permute-done | bytes 524320 | tf_op jit(solution)/shard_map/ppermute | solution.py:379
  165.9 2.4 %collective-permute-start.16 = (f32[256,128]{1,0:T(8,128)S(1)}, f32[256,128]{1,0:T(8,128)S(1)}, u32[]{:S(2)}, u32[]{:S(2)}) collective-permute-start(f32[256,128]{1,0:T(8,128)S(1)} %get-tuple-element.85), channel_id=1, source_target_pairs={{0,4},{2,6},{4,0},{6,2},{8,12},{10,14},{12,8},{14,10},{1,5},{3,7},... | collective-permute-start | bytes 393224 | tf_op jit(solution)/shard_map/ppermute | solution.py:379
  169.0 1.8 collective-permute-start.18
  170.8 2.5 %collective-permute-done.16 = f32[256,128]{1,0:T(8,128)S(1)} collective-permute-done((f32[256,128]{1,0:T(8,128)S(1)}, f32[256,128]{1,0:T(8,128)S(1)}, u32[]{:S(2)}, u32[]{:S(2)}) %collective-permute-start.16) | collective-permute-done | bytes 131104 | tf_op jit(solution)/shard_map/ppermute | solution.py:379
  173.3 7.8 %collective-permute-done.17 = f32[256,128]{1,0:T(8,128)S(1)} collective-permute-done((f32[256,128]{1,0:T(8,128)S(1)}, f32[256,128]{1,0:T(8,128)S(1)}, u32[]{:S(2)}, u32[]{:S(2)}) %collective-permute-start.17) | collective-permute-done | bytes 131104 | tf_op jit(solution)/shard_map/ppermute | solution.py:379
  181.7 2.7 %copy.20 = f32[64,16,4,128]{3,2,1,0:T(4,128)} copy(f32[64,16,4,128]{3,0,2,1:T(8,128)S(1)} %copy_dynamic-update-slice_fusion) | data formatting | bytes 4194304 | tf_op jit(solution)/shard_map/jit(dynamic_update_index_in_dim)/dynamic_update_slice | solution.py:495
  (57 shorter events, 5.1 us)
Async XLA Ops:
  1.7 15.6 %collective-permute-start = (f32[128,256]{1,0:T(8,128)S(1)}, f32[128,256]{1,0:T(8,128)S(1)}, u32[]{:S(2)}, u32[]{:S(2)}) collective-permute-start(f32[128,256]{1,0:T(8,128)S(1)} %fusion), channel_id=1, source_target_pairs={{0,4},{2,6},{4,0},{6,2},{8,12},{10,14},{12,8},{14,10},{1,5},{3,7},... | collective-permute-start | bytes 393224 | tf_op jit(solution)/shard_map/ppermute | solution.py:379
  4.8 12.9 %collective-permute-start.1 = (f32[128,256]{1,0:T(8,128)S(1)}, f32[128,256]{1,0:T(8,128)S(1)}, u32[]{:S(2)}, u32[]{:S(2)}) collective-permute-start(f32[128,256]{1,0:T(8,128)S(1)} %fusion), channel_id=1, source_target_pairs={{0,8},{2,10},{4,12},{6,14},{8,0},{10,2},{12,4},{14,6},{1,9},{3,11}... | collective-permute-start | bytes 393224 | tf_op jit(solution)/shard_map/ppermute | solution.py:379
  7.3 10.3 %collective-permute-start.2 = (f32[128,256]{1,0:T(8,128)S(1)}, f32[128,256]{1,0:T(8,128)S(1)}, u32[]{:S(2)}, u32[]{:S(2)}) collective-permute-start(f32[128,256]{1,0:T(8,128)S(1)} %fusion), channel_id=1, source_target_pairs={{0,12},{2,14},{4,8},{6,10},{8,4},{10,6},{12,0},{14,2},{1,13},{3,15... | collective-permute-start | bytes 393224 | tf_op jit(solution)/shard_map/ppermute | solution.py:379
  17.7 20.6 %copy-start.4 = (f32[512,256]{1,0:T(8,128)}, f32[512,256]{1,0:T(8,128)S(1)}, u32[]{:S(2)}) copy-start(f32[512,256]{1,0:T(8,128)S(1)} %pad_maximum_fusion.near_ref) | copy-start | bytes 1572868
  17.7 4.9 %slice-start = ((f32[512,32,1,256]{3,2,1,0:T(1,128)}), f32[512,1,1,256]{3,2,1,0:T(1,128)S(1)}, s32[]{:S(2)}) async-start(f32[512,32,1,256]{3,2,1,0:T(1,128)} %param.5), calls=%async_computation.3 | async-start | bytes 1048576 | tf_op jit(solution)/shard_map/slice | solution.py:443
  17.8 53.6 %all-to-all-start = ((f32[4,2,512,128]{3,2,1,0:T(8,128)}), f32[4,2,512,128]{3,2,1,0:T(8,128)S(1)}, u32[]{:S(2)}, u32[]{:S(2)}) async-start(f32[4,2,512,128]{3,2,1,0:T(8,128)} %pack.3), calls=%async_computation | async-start | bytes 4194304 | tf_op jit(solution)/shard_map/all_to_all | solution.py:440
  22.6 1.6 copy-start.9
  22.7 16.1 %copy-start.3 = (f32[512,1,1,256]{3,0,2,1:T(8,128)}, f32[512,1,1,256]{3,0,2,1:T(8,128)S(1)}, u32[]{:S(2)}) copy-start(f32[512,1,1,256]{3,0,2,1:T(8,128)S(1)} %copy.38) | copy-start | bytes 1572868
  22.7 12.6 %collective-permute-start.4 = (f32[512,256]{1,0:T(8,128)S(1)}, f32[512,256]{1,0:T(8,128)S(1)}, u32[]{:S(2)}, u32[]{:S(2)}) collective-permute-start(f32[512,256]{1,0:T(8,128)S(1)} %bitcast.72), channel_id=1, source_target_pairs={{0,1},{1,0},{2,3},{3,2},{4,5},{5,4},{6,7},{7,6},{8,9},{9,8},{10,11... | collective-permute-start | bytes 1572872 | tf_op jit(solution)/shard_map/ppermute | solution.py:379
  24.3 26.1 %collective-permute-start.3 = (f32[4,512,128]{2,1,0:T(8,128)S(1)}, f32[4,512,128]{2,1,0:T(8,128)S(1)}, u32[]{:S(2)}, u32[]{:S(2)}) collective-permute-start(f32[4,512,128]{2,1,0:T(8,128)S(1)} %copy-done.9), channel_id=1, source_target_pairs={{0,2},{2,0},{4,6},{6,4},{8,10},{10,8},{12,14},{14,12},{1,3},{3,1},... | collective-permute-start | bytes 3145736 | tf_op jit(solution)/shard_map/ppermute | solution.py:379
  35.3 3.5 %copy-start.11 = (f32[512,256]{1,0:T(8,128)}, f32[512,256]{1,0:T(8,128)S(1)}, u32[]{:S(2)}) copy-start(f32[512,256]{1,0:T(8,128)S(1)} %collective-permute-done.4.far_prior) | copy-start | bytes 1572868
  35.3 26.3 %collective-permute-start.5 = (f32[512,256]{1,0:T(8,128)S(1)}, f32[512,256]{1,0:T(8,128)S(1)}, u32[]{:S(2)}, u32[]{:S(2)}) collective-permute-start(f32[512,256]{1,0:T(8,128)S(1)} %pad_maximum_fusion.near_ref), channel_id=1, source_target_pairs={{0,2},{2,0},{4,6},{6,4},{8,10},{10,8},{12,14},{14,12},{1,3},{3,1},... | collective-permute-start | bytes 1572872 | tf_op jit(solution)/shard_map/ppermute | solution.py:379
  36.8 24.8 %collective-permute-start.6 = (f32[512,256]{1,0:T(8,128)S(1)}, f32[512,256]{1,0:T(8,128)S(1)}, u32[]{:S(2)}, u32[]{:S(2)}) collective-permute-start(f32[512,256]{1,0:T(8,128)S(1)} %pad_maximum_fusion.near_ref), channel_id=1, source_target_pairs={{0,1},{1,0},{2,3},{3,2},{4,5},{5,4},{6,7},{7,6},{8,9},{9,8},{10,11... | collective-permute-start | bytes 1572872 | tf_op jit(solution)/shard_map/ppermute | solution.py:379
  38.3 33.0 %collective-permute-start.7 = (f32[512,256]{1,0:T(8,128)S(1)}, f32[512,256]{1,0:T(8,128)}, u32[]{:S(2)}, u32[]{:S(2)}) collective-permute-start(f32[512,256]{1,0:T(8,128)S(1)} %pad_maximum_fusion.near_ref), channel_id=1, source_target_pairs={{0,3},{1,2},{2,1},{3,0},{4,7},{5,6},{6,5},{7,4},{8,11},{9,10},{10,... | collective-permute-start | bytes 1572872 | tf_op jit(solution)/shard_map/ppermute | solution.py:402
  50.4 1.0 copy-start.10
  61.6 0.8 copy-start.12
  62.4 0.8 copy-start.13
  71.4 1.4 copy-start.1
  72.7 53.4 %all-to-all-start.2 = ((f32[4,2,512,128]{3,2,1,0:T(8,128)}), f32[4,2,512,128]{3,2,1,0:T(8,128)S(1)}, u32[]{:S(2)}, u32[]{:S(2)}) async-start(f32[4,2,512,128]{3,2,1,0:T(8,128)} %pack.5), calls=%async_computation.2 | async-start | bytes 4194304 | tf_op jit(solution)/shard_map/all_to_all | solution.py:440
  77.5 7.6 %copy-start.2 = (f32[4,2,512,128]{3,2,1,0:T(8,128)S(1)}, f32[4,2,512,128]{3,2,1,0:T(8,128)}, u32[]{:S(2)}) copy-start(f32[4,2,512,128]{3,2,1,0:T(8,128)} %copy-done.1) | copy-start | bytes 6291460
  83.6 3.8 %collective-permute-start.8 = (f32[512,512]{1,0:T(8,128)}, f32[512,512]{1,0:T(8,128)S(1)}, u32[]{:S(2)}, u32[]{:S(2)}) collective-permute-start(f32[512,512]{1,0:T(8,128)} %get-tuple-element.63.own_ref), channel_id=1, source_target_pairs={{0,16},{1,17},{2,18},{3,19},{4,20},{5,21},{6,22},{7,23},{8,24},{9,... | collective-permute-start | bytes 3145736 | tf_op jit(solution)/shard_map/ppermute | solution.py:383
  85.2 22.3 %collective-permute-start.9 = (f32[4,512,128]{2,1,0:T(8,128)S(1)}, f32[4,512,128]{2,1,0:T(8,128)S(1)}, u32[]{:S(2)}, u32[]{:S(2)}) collective-permute-start(f32[4,512,128]{2,1,0:T(8,128)S(1)} %slice_bitcast_fusion), channel_id=1, source_target_pairs={{0,2},{2,0},{4,6},{6,4},{8,10},{10,8},{12,14},{14,12},{1,3},{3,1},... | collective-permute-start | bytes 3145736 | tf_op jit(solution)/shard_map/ppermute | solution.py:379
  87.3 1.0 copy-start.6
  107.5 1.0 copy-start.5
  116.4 4.4 %collective-permute-start.10 = (f32[512,512]{1,0:T(8,128)}, f32[512,512]{1,0:T(8,128)S(1)}, u32[]{:S(2)}, u32[]{:S(2)}) collective-permute-start(f32[512,512]{1,0:T(8,128)} %info_part.2.own_ref), channel_id=1, source_target_pairs={{0,16},{1,17},{2,18},{3,19},{4,20},{5,21},{6,22},{7,23},{8,24},{9,... | collective-permute-start | bytes 3145736 | tf_op jit(solution)/shard_map/ppermute | solution.py:383
  120.8 1.0 copy-start.7
  126.1 6.7 %copy-start = (f32[4,2,512,128]{3,2,1,0:T(8,128)}, f32[4,2,512,128]{3,2,1,0:T(8,128)S(1)}, u32[]{:S(2)}) copy-start(f32[4,2,512,128]{3,2,1,0:T(8,128)S(1)} %all-to-all-done.2.far_ref.near_ref) | copy-start | bytes 6291460
  126.1 44.6 %all-to-all-start.1 = ((f32[8,256,128]{2,1,0:T(8,128)}), f32[8,256,128]{2,1,0:T(8,128)S(1)}, u32[]{:S(2)}, u32[]{:S(2)}) async-start(f32[8,256,128]{2,1,0:T(8,128)} %slab_part.1), calls=%async_computation.1 | async-start | bytes 2097152 | tf_op jit(solution)/shard_map/all_to_all | solution.py:478
  140.4 4.5 %collective-permute-start.11 = (f32[512,512]{1,0:T(8,128)}, f32[512,512]{1,0:T(8,128)S(1)}, u32[]{:S(2)}, u32[]{:S(2)}) collective-permute-start(f32[512,512]{1,0:T(8,128)} %info_part.3.own_ref), channel_id=1, source_target_pairs={{0,16},{1,17},{2,18},{3,19},{4,20},{5,21},{6,22},{7,23},{8,24},{9,... | collective-permute-start | bytes 3145736 | tf_op jit(solution)/shard_map/ppermute | solution.py:383
  144.9 1.0 copy-start.8
  150.3 15.5 %collective-permute-start.15 = (f32[4,256,128]{2,1,0:T(8,128)}, f32[4,256,128]{2,1,0:T(8,128)S(1)}, u32[]{:S(2)}, u32[]{:S(2)}) collective-permute-start(f32[4,256,128]{2,1,0:T(8,128)} %get-tuple-element.73), channel_id=1, source_target_pairs={{0,2},{2,0},{4,6},{6,4},{8,10},{10,8},{12,14},{14,12},{1,3},{3,1},... | collective-permute-start | bytes 1572872 | tf_op jit(solution)/shard_map/ppermute | solution.py:379
  153.2 15.7 %collective-permute-start.12 = (f32[256,128]{1,0:T(8,128)S(1)}, f32[256,128]{1,0:T(8,128)S(1)}, u32[]{:S(2)}, u32[]{:S(2)}) collective-permute-start(f32[256,128]{1,0:T(8,128)S(1)} %get-tuple-element.89), channel_id=1, source_target_pairs={{0,4},{2,6},{4,0},{6,2},{8,12},{10,14},{12,8},{14,10},{1,5},{3,7},... | collective-permute-start | bytes 393224 | tf_op jit(solution)/shard_map/ppermute | solution.py:379
  154.8 16.0 %collective-permute-start.13 = (f32[256,128]{1,0:T(8,128)S(1)}, f32[256,128]{1,0:T(8,128)S(1)}, u32[]{:S(2)}, u32[]{:S(2)}) collective-permute-start(f32[256,128]{1,0:T(8,128)S(1)} %get-tuple-element.88), channel_id=1, source_target_pairs={{0,8},{2,10},{4,12},{6,14},{8,0},{10,2},{12,4},{14,6},{1,9},{3,11}... | collective-permute-start | bytes 393224 | tf_op jit(solution)/shard_map/ppermute | solution.py:379
  157.1 13.6 %collective-permute-start.14 = (f32[256,128]{1,0:T(8,128)S(1)}, f32[256,128]{1,0:T(8,128)S(1)}, u32[]{:S(2)}, u32[]{:S(2)}) collective-permute-start(f32[256,128]{1,0:T(8,128)S(1)} %get-tuple-element.87), channel_id=1, source_target_pairs={{0,12},{2,14},{4,8},{6,10},{8,4},{10,6},{12,0},{14,2},{1,13},{3,15... | collective-permute-start | bytes 393224 | tf_op jit(solution)/shard_map/ppermute | solution.py:379
  165.9 7.4 %collective-permute-start.16 = (f32[256,128]{1,0:T(8,128)S(1)}, f32[256,128]{1,0:T(8,128)S(1)}, u32[]{:S(2)}, u32[]{:S(2)}) collective-permute-start(f32[256,128]{1,0:T(8,128)S(1)} %get-tuple-element.85), channel_id=1, source_target_pairs={{0,4},{2,6},{4,0},{6,2},{8,12},{10,14},{12,8},{14,10},{1,5},{3,7},... | collective-permute-start | bytes 393224 | tf_op jit(solution)/shard_map/ppermute | solution.py:379
  168.3 12.8 %collective-permute-start.17 = (f32[256,128]{1,0:T(8,128)S(1)}, f32[256,128]{1,0:T(8,128)S(1)}, u32[]{:S(2)}, u32[]{:S(2)}) collective-permute-start(f32[256,128]{1,0:T(8,128)S(1)} %get-tuple-element.84), channel_id=1, source_target_pairs={{0,8},{2,10},{4,12},{6,14},{8,0},{10,2},{12,4},{14,6},{1,9},{3,11}... | collective-permute-start | bytes 393224 | tf_op jit(solution)/shard_map/ppermute | solution.py:379
  169.0 12.1 %collective-permute-start.18 = (f32[256,128]{1,0:T(8,128)S(1)}, f32[256,128]{1,0:T(8,128)S(1)}, u32[]{:S(2)}, u32[]{:S(2)}) collective-permute-start(f32[256,128]{1,0:T(8,128)S(1)} %get-tuple-element.83), channel_id=1, source_target_pairs={{0,12},{2,14},{4,8},{6,10},{8,4},{10,6},{12,0},{14,2},{1,13},{3,15... | collective-permute-start | bytes 393224 | tf_op jit(solution)/shard_map/ppermute | solution.py:379

commit v3 on v2

--- a/solution.py
+++ b/solution.py
@@ -477,13 +477,12 @@
             slab = slab_part(rows, spots[part], inverse, info, other)
             slab = lax.all_to_all(slab, "row", 0, 0, tiled=True)
             continue
-        sides = list(slab_sides(rows, spots[part], inverse, info, other))
-        sides[1] = swapped(sides[1], "row", 1)
+        sides = slab_sides(rows, spots[part], inverse, info, other)
         placed = []
         for change, side in enumerate(sides):
             for k in range(rows // 2):
                 piece = lax.dynamic_index_in_dim(side, (row // 2) ^ k, 0, keepdims=False)
-                piece = swapped(piece, "row", 2 * k) if k else piece
+                piece = swapped(piece, "row", 2 * k + change) if 2 * k + change else piece
                 placed.append((row ^ (2 * k + change), piece.reshape(total // rows, each, LANES)))
         slab, received = lax.optimization_barrier((slab, [piece for _, piece in placed]))
         placed = [(source, piece) for (source, _), piece in zip(placed, received)]

time: 185 us -> 184 us (level)
  waiting for transfers between devices: 50.7 us -> 44 us
  starting transfers between devices: 46.1 us -> 50.2 us
    ppermute x15, waiting for transfers between devices: 37.1 us -> 30.5 us  [swapped(): return lax.ppermute(value, axis, [(i, i ^ bits) for i in range(count)])]
    ppermute x15, starting transfers between devices: 24.4 us -> 28.5 us  [swapped(): return lax.ppermute(value, axis, [(i, i ^ bits) for i in range(count)])]
  transfers between devices with their start and end apart: 22 -> 22, of which waited for: 12 -> 12; matrix products, arithmetic and copies ran while one was open for 1% -> 2% of each run, Pallas kernels for 39% -> 39%
where the time goes in v3:
time: 184 us; the launch traced here: 183 us
  Pallas kernels  72 us (39%)
  starting transfers between devices  50.2 us (27%)
  waiting for transfers between devices  44 us (24%)
  local copies, waits for them, and re-layouts  15.7 us (9%)
    ppermute x15, waiting for transfers between devices, swapped(): return lax.ppermute(value, axis, [(i, i ^ bits) for i in range(count)])  30.5 us
    ppermute x15, starting transfers between devices, swapped(): return lax.ppermute(value, axis, [(i, i ^ bits) for i in range(count)])  28.5 us
    pallas_call x1, Pallas kernels, factor(): pl.pallas_call(factor_kernel, out_shape=shape_of(size, size), in_specs=[v...  18.8 us
    pallas_call x2, Pallas kernels, info_part(): pl.pallas_call(functools.partial(info_kernel, each), out_shape=shape_of(t...  15.5 us
    pallas_call x3, Pallas kernels, pack(): pl.pallas_call(functools.partial(pack_kernel, part * each, each, swapped_...  14 us
    all_to_all x2, starting transfers between devices, over(): lax.all_to_all(piece, 'row', 0, 0, axis_index_groups=same_side, tiled=True)  9.68 us
    pallas_call x1, Pallas kernels, prior_part(): pl.pallas_call(functools.partial(prior_kernel, chunk), out_shape=out, gri...  8.77 us
    ppermute x1, waiting for transfers between devices, all_panels(): far = [swapped(near, 'col', 1), lax.ppermute(near, ('row', 'col'), order)]  8.14 us
  transfers between devices with their start and end apart: 22, of which 12 were waited for; matrix products, arithmetic and copies ran while one was open for 2% of the time, Pallas kernels for 39%

profile of v3, /device:TPU:0, one launch (start us, length us, event | category | flops | bytes accessed | tf_op | source)
XLA Modules:
  0.0 182.9 jit_solution(6206480651964312081)
XLA Ops:
  0.0 0.9 slice.38
  1.7 3.1 %collective-permute-start = (f32[128,256]{1,0:T(8,128)S(1)}, f32[128,256]{1,0:T(8,128)S(1)}, u32[]{:S(2)}, u32[]{:S(2)}) collective-permute-start(f32[128,256]{1,0:T(8,128)S(1)} %fusion), channel_id=1, source_target_pairs={{0,4},{2,6},{4,0},{6,2},{8,12},{10,14},{12,8},{14,10},{1,5},{3,7},... | collective-permute-start | bytes 393224 | tf_op jit(solution)/shard_map/ppermute | solution.py:379
  4.8 2.6 %collective-permute-start.1 = (f32[128,256]{1,0:T(8,128)S(1)}, f32[128,256]{1,0:T(8,128)S(1)}, u32[]{:S(2)}, u32[]{:S(2)}) collective-permute-start(f32[128,256]{1,0:T(8,128)S(1)} %fusion), channel_id=1, source_target_pairs={{0,8},{2,10},{4,12},{6,14},{8,0},{10,2},{12,4},{14,6},{1,9},{3,11}... | collective-permute-start | bytes 393224 | tf_op jit(solution)/shard_map/ppermute | solution.py:379
  8.0 5.0 %pack.3 = f32[4,2,512,128]{3,2,1,0:T(8,128)} custom-call(s32[10]{0:T(128)} %stack.63.spot_ref, f32[128,8,8,128]{3,2,1,0:T(8,128)} %bitcast.66, f32[128,8,8,128]{3,2,1,0:T(8,128)} %bitcast.67), custom_call_target="tpu_custom_call" | custom-call | tf_op jit(solution)/shard_map/pack/pallas_call | solution.py:259
  13.0 4.3 %pack.4 = f32[4,512,128]{2,1,0:T(8,128)} custom-call(s32[10]{0:T(128)} %stack.63.spot_ref, f32[128,8,8,128]{3,2,1,0:T(8,128)} %bitcast.68), custom_call_target="tpu_custom_call" | custom-call | tf_op jit(solution)/shard_map/pack/pallas_call | solution.py:259
  17.8 4.9 %all-to-all-start = ((f32[4,2,512,128]{3,2,1,0:T(8,128)}), f32[4,2,512,128]{3,2,1,0:T(8,128)S(1)}, u32[]{:S(2)}, u32[]{:S(2)}) async-start(f32[4,2,512,128]{3,2,1,0:T(8,128)} %pack.3), calls=%async_computation | async-start | bytes 4194304 | tf_op jit(solution)/shard_map/all_to_all | solution.py:440
  22.7 1.6 collective-permute-start.4
  24.3 1.5 collective-permute-start.3
  25.8 9.5 %collective-permute-done.4.far_prior = f32[512,256]{1,0:T(8,128)S(1)} collective-permute-done((f32[512,256]{1,0:T(8,128)S(1)}, f32[512,256]{1,0:T(8,128)S(1)}, u32[]{:S(2)}, u32[]{:S(2)}) %collective-permute-start.4) | collective-permute-done | bytes 524320 | tf_op jit(solution)/shard_map/ppermute | solution.py:379
  35.3 1.5 collective-permute-start.5
  36.8 1.5 collective-permute-start.6
  38.8 8.8 %prior_part.1 = (f32[512,1024]{1,0:T(8,128)}, f32[512,512]{1,0:T(8,128)}) custom-call(s32[10]{0:T(128)} %stack.63.spot_ref, f32[512,256]{1,0:T(8,128)} %bitcast.75, f32[512,256]{1,0:T(8,128)} %copy-done.11, f32[512,8,8,128]{3,2,1,0:T(8,128)} %bitcast.70), custom_call_target="tpu_custom_call" | custom-call | tf_op jit(solution)/shard_map/prior_part/pallas_call | solution.py:169
  47.6 2.8 %collective-permute-done.3.refs_0_ = f32[4,512,128]{2,1,0:T(8,128)S(1)} collective-permute-done((f32[4,512,128]{2,1,0:T(8,128)S(1)}, f32[4,512,128]{2,1,0:T(8,128)S(1)}, u32[]{:S(2)}, u32[]{:S(2)}) %collective-permute-start.3) | collective-permute-done | bytes 1048608 | tf_op jit(solution)/shard_map/ppermute | solution.py:379
  50.4 1.0 copy-done.10
  51.4 4.7 %pack.5 = f32[4,2,512,128]{3,2,1,0:T(8,128)} custom-call(s32[10]{0:T(128)} %stack.63.spot_ref, f32[4,512,128]{2,1,0:T(8,128)} %copy-done.10, f32[128,8,8,128]{3,2,1,0:T(8,128)} %bitcast.69), custom_call_target="tpu_custom_call" | custom-call | tf_op jit(solution)/shard_map/pack/pallas_call | solution.py:259
  56.1 5.5 %collective-permute-done.5.near_next = f32[512,256]{1,0:T(8,128)S(1)} collective-permute-done((f32[512,256]{1,0:T(8,128)S(1)}, f32[512,256]{1,0:T(8,128)S(1)}, u32[]{:S(2)}, u32[]{:S(2)}) %collective-permute-start.5) | collective-permute-done | bytes 524320 | tf_op jit(solution)/shard_map/ppermute | solution.py:379
  63.2 8.1 %collective-permute-done.7.far_next = f32[512,256]{1,0:T(8,128)} collective-permute-done((f32[512,256]{1,0:T(8,128)S(1)}, f32[512,256]{1,0:T(8,128)}, u32[]{:S(2)}, u32[]{:S(2)}) %collective-permute-start.7) | collective-permute-done | bytes 524320 | tf_op jit(solution)/shard_map/ppermute | solution.py:402
  71.4 1.4 copy-done.1
  72.7 4.8 %all-to-all-start.2 = ((f32[4,2,512,128]{3,2,1,0:T(8,128)}), f32[4,2,512,128]{3,2,1,0:T(8,128)S(1)}, u32[]{:S(2)}, u32[]{:S(2)}) async-start(f32[4,2,512,128]{3,2,1,0:T(8,128)} %pack.5), calls=%async_computation.2 | async-start | bytes 4194304 | tf_op jit(solution)/shard_map/all_to_all | solution.py:440
  77.5 6.0 %panel_gram.1 = (f32[1024,512]{1,0:T(8,128)}, f32[512,512]{1,0:T(8,128)}) custom-call(s32[10]{0:T(128)} %stack.63.spot_ref, f32[512,256]{1,0:T(8,128)} %copy-done.4, f32[512,256]{1,0:T(8,128)} %copy-done.12, f32[512,256]{1,0:T(8,128)} %copy-done.13, f32[512,256]{1,0:T(8,128)} %collective-permute-done.7.far_next, f32[512,512]{1,0:T(8,128)} %get-tuple-element.61.prior_ref), custom_call_target="tpu_custom_call" | custom-call | tf_op jit(solution)/shard_map/panel_gram/pallas_call | solution.py:213
  83.6 1.5 collective-permute-start.8
  85.2 1.6 collective-permute-start.9
  87.3 1.0 copy-done.6
  88.3 18.8 %factor.1.inverse_ref = f32[512,512]{1,0:T(8,128)} custom-call(f32[512,512]{1,0:T(8,128)} %get-tuple-element.63.own_ref, f32[512,512]{1,0:T(8,128)} %copy-done.6), custom_call_target="tpu_custom_call" | custom-call | tf_op jit(solution)/shard_map/factor/pallas_call | solution.py:133
  107.5 1.0 copy-done.5
  108.5 7.9 %info_part.2.own_ref = f32[512,512]{1,0:T(8,128)} custom-call(s32[10]{0:T(128)} %stack.63.spot_ref, f32[1024,512]{1,0:T(8,128)} %get-tuple-element.69.rows_ref, f32[512,1024]{1,0:T(8,128)} %get-tuple-element.66.prior_ref, f32[4,512,128]{2,1,0:T(8,128)} %copy-done.5, f32[4,2,512,128]{3,2,1,0:T(8,128)} %copy-done.1), custom_call_target="tpu_custom_call" | custom-call | tf_op jit(solution)/shard_map/info_part/pallas_call | solution.py:292
  116.4 2.0 %collective-permute-start.10 = (f32[512,512]{1,0:T(8,128)}, f32[512,512]{1,0:T(8,128)S(1)}, u32[]{:S(2)}, u32[]{:S(2)}) collective-permute-start(f32[512,512]{1,0:T(8,128)} %info_part.2.own_ref), channel_id=1, source_target_pairs={{0,16},{1,17},{2,18},{3,19},{4,20},{5,21},{6,22},{7,23},{8,24},{9,... | collective-permute-start | bytes 3145736 | tf_op jit(solution)/shard_map/ppermute | solution.py:383
  118.4 2.4 %collective-permute-done.10.other_ref = f32[512,512]{1,0:T(8,128)S(1)} collective-permute-done((f32[512,512]{1,0:T(8,128)}, f32[512,512]{1,0:T(8,128)S(1)}, u32[]{:S(2)}, u32[]{:S(2)}) %collective-permute-start.10) | collective-permute-done | bytes 1048608 | tf_op jit(solution)/shard_map/ppermute | solution.py:383
  120.8 1.0 copy-done.7
  121.8 4.4 %slab_part.1 = f32[8,256,128]{2,1,0:T(8,128)} custom-call(s32[10]{0:T(128)} %stack.63.spot_ref, f32[512,512]{1,0:T(8,128)} %factor.1.inverse_ref, f32[512,512]{1,0:T(8,128)} %info_part.2.own_ref, f32[512,512]{1,0:T(8,128)} %copy-done.7), custom_call_target="tpu_custom_call" | custom-call | tf_op jit(solution)/shard_map/slab_part/pallas_call | solution.py:333
  126.1 6.0 %all-to-all-start.1 = ((f32[8,256,128]{2,1,0:T(8,128)}), f32[8,256,128]{2,1,0:T(8,128)S(1)}, u32[]{:S(2)}, u32[]{:S(2)}) async-start(f32[8,256,128]{2,1,0:T(8,128)} %slab_part.1), calls=%async_computation.1 | async-start | bytes 2097152 | tf_op jit(solution)/shard_map/all_to_all | solution.py:478
  132.8 7.6 %info_part.3.own_ref = f32[512,512]{1,0:T(8,128)} custom-call(s32[10]{0:T(128)} %stack.70.spot_ref, f32[1024,512]{1,0:T(8,128)} %get-tuple-element.69.rows_ref, f32[512,1024]{1,0:T(8,128)} %get-tuple-element.66.prior_ref, f32[4,2,512,128]{3,2,1,0:T(8,128)} %copy-done, f32[4,2,512,128]{3,2,1,0:T(8,128)} %copy-done), custom_call_target="tpu_custom_call" | custom-call | tf_op jit(solution)/shard_map/info_part/pallas_call | solution.py:292
  140.4 2.0 %collective-permute-start.11 = (f32[512,512]{1,0:T(8,128)}, f32[512,512]{1,0:T(8,128)S(1)}, u32[]{:S(2)}, u32[]{:S(2)}) collective-permute-start(f32[512,512]{1,0:T(8,128)} %info_part.3.own_ref), channel_id=1, source_target_pairs={{0,16},{1,17},{2,18},{3,19},{4,20},{5,21},{6,22},{7,23},{8,24},{9,... | collective-permute-start | bytes 3145736 | tf_op jit(solution)/shard_map/ppermute | solution.py:383
  142.5 2.4 %collective-permute-done.11.other_ref = f32[512,512]{1,0:T(8,128)S(1)} collective-permute-done((f32[512,512]{1,0:T(8,128)}, f32[512,512]{1,0:T(8,128)S(1)}, u32[]{:S(2)}, u32[]{:S(2)}) %collective-permute-start.11) | collective-permute-done | bytes 1048608 | tf_op jit(solution)/shard_map/ppermute | solution.py:383
  144.9 1.0 copy-done.8
  145.9 4.5 %slab_sides.1 = (f32[4,256,128]{2,1,0:T(8,128)}, f32[4,256,128]{2,1,0:T(8,128)}) custom-call(s32[10]{0:T(128)} %stack.70.spot_ref, f32[512,512]{1,0:T(8,128)} %factor.1.inverse_ref, f32[512,512]{1,0:T(8,128)} %info_part.3.own_ref, f32[512,512]{1,0:T(8,128)} %copy-done.8), custom_call_target="tpu_custom_call" | custom-call | tf_op jit(solution)/shard_map/slab_sides/pallas_call | solution.py:366
  150.3 1.1 dynamic-slice_bitcast_fusion
  151.5 1.8 collective-permute-start.15
  153.3 1.5 collective-permute-start.16
  154.8 3.3 %collective-permute-start.17 = (f32[256,128]{1,0:T(8,128)S(1)}, f32[256,128]{1,0:T(8,128)S(1)}, u32[]{:S(2)}, u32[]{:S(2)}) collective-permute-start(f32[256,128]{1,0:T(8,128)S(1)} %get-tuple-element.84), channel_id=1, source_target_pairs={{0,10},{2,8},{4,14},{6,12},{8,2},{10,0},{12,6},{14,4},{1,11},{3,9}... | collective-permute-start | bytes 393224 | tf_op jit(solution)/shard_map/ppermute | solution.py:379
  158.3 1.1 dynamic-slice_bitcast_fusion.4
  159.4 0.9 collective-permute-start.12
  160.3 5.1 %collective-permute-start.13 = (f32[256,128]{1,0:T(8,128)S(1)}, f32[256,128]{1,0:T(8,128)S(1)}, u32[]{:S(2)}, u32[]{:S(2)}) collective-permute-start(f32[256,128]{1,0:T(8,128)S(1)} %get-tuple-element.88), channel_id=1, source_target_pairs={{0,8},{2,10},{4,12},{6,14},{8,0},{10,2},{12,4},{14,6},{1,9},{3,11}... | collective-permute-start | bytes 393224 | tf_op jit(solution)/shard_map/ppermute | solution.py:379
  165.5 2.3 %collective-permute-start.14 = (f32[256,128]{1,0:T(8,128)S(1)}, f32[256,128]{1,0:T(8,128)S(1)}, u32[]{:S(2)}, u32[]{:S(2)}) collective-permute-start(f32[256,128]{1,0:T(8,128)S(1)} %get-tuple-element.87), channel_id=1, source_target_pairs={{0,12},{2,14},{4,8},{6,10},{8,4},{10,6},{12,0},{14,2},{1,13},{3,15... | collective-permute-start | bytes 393224 | tf_op jit(solution)/shard_map/ppermute | solution.py:379
  167.8 0.9 collective-permute-done.17
  168.6 1.1 collective-permute-done.12
  169.7 9.9 %collective-permute-done.13 = f32[256,128]{1,0:T(8,128)S(1)} collective-permute-done((f32[256,128]{1,0:T(8,128)S(1)}, f32[256,128]{1,0:T(8,128)S(1)}, u32[]{:S(2)}, u32[]{:S(2)}) %collective-permute-start.13) | collective-permute-done | bytes 131104 | tf_op jit(solution)/shard_map/ppermute | solution.py:379
  180.3 2.7 %copy.20 = f32[64,16,4,128]{3,2,1,0:T(4,128)} copy(f32[64,16,4,128]{3,0,2,1:T(8,128)S(1)} %copy_dynamic-update-slice_fusion) | data formatting | bytes 4194304 | tf_op jit(solution)/shard_map/jit(dynamic_update_index_in_dim)/dynamic_update_slice | solution.py:494
  (57 shorter events, 5.8 us)
Async XLA Ops:
  1.7 15.6 %collective-permute-start = (f32[128,256]{1,0:T(8,128)S(1)}, f32[128,256]{1,0:T(8,128)S(1)}, u32[]{:S(2)}, u32[]{:S(2)}) collective-permute-start(f32[128,256]{1,0:T(8,128)S(1)} %fusion), channel_id=1, source_target_pairs={{0,4},{2,6},{4,0},{6,2},{8,12},{10,14},{12,8},{14,10},{1,5},{3,7},... | collective-permute-start | bytes 393224 | tf_op jit(solution)/shard_map/ppermute | solution.py:379
  4.8 12.9 %collective-permute-start.1 = (f32[128,256]{1,0:T(8,128)S(1)}, f32[128,256]{1,0:T(8,128)S(1)}, u32[]{:S(2)}, u32[]{:S(2)}) collective-permute-start(f32[128,256]{1,0:T(8,128)S(1)} %fusion), channel_id=1, source_target_pairs={{0,8},{2,10},{4,12},{6,14},{8,0},{10,2},{12,4},{14,6},{1,9},{3,11}... | collective-permute-start | bytes 393224 | tf_op jit(solution)/shard_map/ppermute | solution.py:379
  7.3 10.3 %collective-permute-start.2 = (f32[128,256]{1,0:T(8,128)S(1)}, f32[128,256]{1,0:T(8,128)S(1)}, u32[]{:S(2)}, u32[]{:S(2)}) collective-permute-start(f32[128,256]{1,0:T(8,128)S(1)} %fusion), channel_id=1, source_target_pairs={{0,12},{2,14},{4,8},{6,10},{8,4},{10,6},{12,0},{14,2},{1,13},{3,15... | collective-permute-start | bytes 393224 | tf_op jit(solution)/shard_map/ppermute | solution.py:379
  17.7 20.6 %copy-start.4 = (f32[512,256]{1,0:T(8,128)}, f32[512,256]{1,0:T(8,128)S(1)}, u32[]{:S(2)}) copy-start(f32[512,256]{1,0:T(8,128)S(1)} %pad_maximum_fusion.near_ref) | copy-start | bytes 1572868
  17.7 4.9 %slice-start = ((f32[512,32,1,256]{3,2,1,0:T(1,128)}), f32[512,1,1,256]{3,2,1,0:T(1,128)S(1)}, s32[]{:S(2)}) async-start(f32[512,32,1,256]{3,2,1,0:T(1,128)} %param.5), calls=%async_computation.3 | async-start | bytes 1048576 | tf_op jit(solution)/shard_map/slice | solution.py:443
  17.8 53.6 %all-to-all-start = ((f32[4,2,512,128]{3,2,1,0:T(8,128)}), f32[4,2,512,128]{3,2,1,0:T(8,128)S(1)}, u32[]{:S(2)}, u32[]{:S(2)}) async-start(f32[4,2,512,128]{3,2,1,0:T(8,128)} %pack.3), calls=%async_computation | async-start | bytes 4194304 | tf_op jit(solution)/shard_map/all_to_all | solution.py:440
  22.6 1.6 copy-start.9
  22.7 16.1 %copy-start.3 = (f32[512,1,1,256]{3,0,2,1:T(8,128)}, f32[512,1,1,256]{3,0,2,1:T(8,128)S(1)}, u32[]{:S(2)}) copy-start(f32[512,1,1,256]{3,0,2,1:T(8,128)S(1)} %copy.38) | copy-start | bytes 1572868
  22.7 12.6 %collective-permute-start.4 = (f32[512,256]{1,0:T(8,128)S(1)}, f32[512,256]{1,0:T(8,128)S(1)}, u32[]{:S(2)}, u32[]{:S(2)}) collective-permute-start(f32[512,256]{1,0:T(8,128)S(1)} %bitcast.74), channel_id=1, source_target_pairs={{0,1},{1,0},{2,3},{3,2},{4,5},{5,4},{6,7},{7,6},{8,9},{9,8},{10,11... | collective-permute-start | bytes 1572872 | tf_op jit(solution)/shard_map/ppermute | solution.py:379
  24.3 26.1 %collective-permute-start.3 = (f32[4,512,128]{2,1,0:T(8,128)S(1)}, f32[4,512,128]{2,1,0:T(8,128)S(1)}, u32[]{:S(2)}, u32[]{:S(2)}) collective-permute-start(f32[4,512,128]{2,1,0:T(8,128)S(1)} %copy-done.9), channel_id=1, source_target_pairs={{0,2},{2,0},{4,6},{6,4},{8,10},{10,8},{12,14},{14,12},{1,3},{3,1},... | collective-permute-start | bytes 3145736 | tf_op jit(solution)/shard_map/ppermute | solution.py:379
  35.3 3.5 %copy-start.11 = (f32[512,256]{1,0:T(8,128)}, f32[512,256]{1,0:T(8,128)S(1)}, u32[]{:S(2)}) copy-start(f32[512,256]{1,0:T(8,128)S(1)} %collective-permute-done.4.far_prior) | copy-start | bytes 1572868
  35.3 26.3 %collective-permute-start.5 = (f32[512,256]{1,0:T(8,128)S(1)}, f32[512,256]{1,0:T(8,128)S(1)}, u32[]{:S(2)}, u32[]{:S(2)}) collective-permute-start(f32[512,256]{1,0:T(8,128)S(1)} %pad_maximum_fusion.near_ref), channel_id=1, source_target_pairs={{0,2},{2,0},{4,6},{6,4},{8,10},{10,8},{12,14},{14,12},{1,3},{3,1},... | collective-permute-start | bytes 1572872 | tf_op jit(solution)/shard_map/ppermute | solution.py:379
  36.8 24.8 %collective-permute-start.6 = (f32[512,256]{1,0:T(8,128)S(1)}, f32[512,256]{1,0:T(8,128)S(1)}, u32[]{:S(2)}, u32[]{:S(2)}) collective-permute-start(f32[512,256]{1,0:T(8,128)S(1)} %pad_maximum_fusion.near_ref), channel_id=1, source_target_pairs={{0,1},{1,0},{2,3},{3,2},{4,5},{5,4},{6,7},{7,6},{8,9},{9,8},{10,11... | collective-permute-start | bytes 1572872 | tf_op jit(solution)/shard_map/ppermute | solution.py:379
  38.3 33.0 %collective-permute-start.7 = (f32[512,256]{1,0:T(8,128)S(1)}, f32[512,256]{1,0:T(8,128)}, u32[]{:S(2)}, u32[]{:S(2)}) collective-permute-start(f32[512,256]{1,0:T(8,128)S(1)} %pad_maximum_fusion.near_ref), channel_id=1, source_target_pairs={{0,3},{1,2},{2,1},{3,0},{4,7},{5,6},{6,5},{7,4},{8,11},{9,10},{10,... | collective-permute-start | bytes 1572872 | tf_op jit(solution)/shard_map/ppermute | solution.py:402
  50.4 1.0 copy-start.10
  61.6 0.8 copy-start.12
  62.4 0.8 copy-start.13
  71.4 1.4 copy-start.1
  72.7 53.4 %all-to-all-start.2 = ((f32[4,2,512,128]{3,2,1,0:T(8,128)}), f32[4,2,512,128]{3,2,1,0:T(8,128)S(1)}, u32[]{:S(2)}, u32[]{:S(2)}) async-start(f32[4,2,512,128]{3,2,1,0:T(8,128)} %pack.5), calls=%async_computation.2 | async-start | bytes 4194304 | tf_op jit(solution)/shard_map/all_to_all | solution.py:440
  77.5 7.6 %copy-start.2 = (f32[4,2,512,128]{3,2,1,0:T(8,128)S(1)}, f32[4,2,512,128]{3,2,1,0:T(8,128)}, u32[]{:S(2)}) copy-start(f32[4,2,512,128]{3,2,1,0:T(8,128)} %copy-done.1) | copy-start | bytes 6291460
  83.6 3.8 %collective-permute-start.8 = (f32[512,512]{1,0:T(8,128)}, f32[512,512]{1,0:T(8,128)S(1)}, u32[]{:S(2)}, u32[]{:S(2)}) collective-permute-start(f32[512,512]{1,0:T(8,128)} %get-tuple-element.63.own_ref), channel_id=1, source_target_pairs={{0,16},{1,17},{2,18},{3,19},{4,20},{5,21},{6,22},{7,23},{8,24},{9,... | collective-permute-start | bytes 3145736 | tf_op jit(solution)/shard_map/ppermute | solution.py:383
  85.2 22.3 %collective-permute-start.9 = (f32[4,512,128]{2,1,0:T(8,128)S(1)}, f32[4,512,128]{2,1,0:T(8,128)S(1)}, u32[]{:S(2)}, u32[]{:S(2)}) collective-permute-start(f32[4,512,128]{2,1,0:T(8,128)S(1)} %slice_bitcast_fusion), channel_id=1, source_target_pairs={{0,2},{2,0},{4,6},{6,4},{8,10},{10,8},{12,14},{14,12},{1,3},{3,1},... | collective-permute-start | bytes 3145736 | tf_op jit(solution)/shard_map/ppermute | solution.py:379
  87.3 1.0 copy-start.6
  107.5 1.0 copy-start.5
  116.4 4.4 %collective-permute-start.10 = (f32[512,512]{1,0:T(8,128)}, f32[512,512]{1,0:T(8,128)S(1)}, u32[]{:S(2)}, u32[]{:S(2)}) collective-permute-start(f32[512,512]{1,0:T(8,128)} %info_part.2.own_ref), channel_id=1, source_target_pairs={{0,16},{1,17},{2,18},{3,19},{4,20},{5,21},{6,22},{7,23},{8,24},{9,... | collective-permute-start | bytes 3145736 | tf_op jit(solution)/shard_map/ppermute | solution.py:383
  120.8 1.0 copy-start.7
  126.1 6.7 %copy-start = (f32[4,2,512,128]{3,2,1,0:T(8,128)}, f32[4,2,512,128]{3,2,1,0:T(8,128)S(1)}, u32[]{:S(2)}) copy-start(f32[4,2,512,128]{3,2,1,0:T(8,128)S(1)} %all-to-all-done.2.far_ref.near_ref) | copy-start | bytes 6291460
  126.1 41.6 %all-to-all-start.1 = ((f32[8,256,128]{2,1,0:T(8,128)}), f32[8,256,128]{2,1,0:T(8,128)S(1)}, u32[]{:S(2)}, u32[]{:S(2)}) async-start(f32[8,256,128]{2,1,0:T(8,128)} %slab_part.1), calls=%async_computation.1 | async-start | bytes 2097152 | tf_op jit(solution)/shard_map/all_to_all | solution.py:478
  140.4 4.5 %collective-permute-start.11 = (f32[512,512]{1,0:T(8,128)}, f32[512,512]{1,0:T(8,128)S(1)}, u32[]{:S(2)}, u32[]{:S(2)}) collective-permute-start(f32[512,512]{1,0:T(8,128)} %info_part.3.own_ref), channel_id=1, source_target_pairs={{0,16},{1,17},{2,18},{3,19},{4,20},{5,21},{6,22},{7,23},{8,24},{9,... | collective-permute-start | bytes 3145736 | tf_op jit(solution)/shard_map/ppermute | solution.py:383
  144.9 1.0 copy-start.8
  151.5 8.9 %collective-permute-start.15 = (f32[256,128]{1,0:T(8,128)S(1)}, f32[256,128]{1,0:T(8,128)S(1)}, u32[]{:S(2)}, u32[]{:S(2)}) collective-permute-start(f32[256,128]{1,0:T(8,128)S(1)} %get-tuple-element.86), channel_id=1, source_target_pairs={{0,2},{2,0},{4,6},{6,4},{8,10},{10,8},{12,14},{14,12},{1,3},{3,1},... | collective-permute-start | bytes 393224 | tf_op jit(solution)/shard_map/ppermute | solution.py:379
  153.3 12.2 %collective-permute-start.16 = (f32[256,128]{1,0:T(8,128)S(1)}, f32[256,128]{1,0:T(8,128)S(1)}, u32[]{:S(2)}, u32[]{:S(2)}) collective-permute-start(f32[256,128]{1,0:T(8,128)S(1)} %get-tuple-element.85), channel_id=1, source_target_pairs={{0,6},{2,4},{4,2},{6,0},{8,14},{10,12},{12,10},{14,8},{1,7},{3,5},... | collective-permute-start | bytes 393224 | tf_op jit(solution)/shard_map/ppermute | solution.py:379
  154.8 13.9 %collective-permute-start.17 = (f32[256,128]{1,0:T(8,128)S(1)}, f32[256,128]{1,0:T(8,128)S(1)}, u32[]{:S(2)}, u32[]{:S(2)}) collective-permute-start(f32[256,128]{1,0:T(8,128)S(1)} %get-tuple-element.84), channel_id=1, source_target_pairs={{0,10},{2,8},{4,14},{6,12},{8,2},{10,0},{12,6},{14,4},{1,11},{3,9}... | collective-permute-start | bytes 393224 | tf_op jit(solution)/shard_map/ppermute | solution.py:379
  158.0 10.6 %collective-permute-start.18 = (f32[256,128]{1,0:T(8,128)S(1)}, f32[256,128]{1,0:T(8,128)S(1)}, u32[]{:S(2)}, u32[]{:S(2)}) collective-permute-start(f32[256,128]{1,0:T(8,128)S(1)} %get-tuple-element.83), channel_id=1, source_target_pairs={{0,14},{2,12},{4,10},{6,8},{8,6},{10,4},{12,2},{14,0},{1,15},{3,13... | collective-permute-start | bytes 393224 | tf_op jit(solution)/shard_map/ppermute | solution.py:379
  159.4 10.3 %collective-permute-start.12 = (f32[256,128]{1,0:T(8,128)S(1)}, f32[256,128]{1,0:T(8,128)S(1)}, u32[]{:S(2)}, u32[]{:S(2)}) collective-permute-start(f32[256,128]{1,0:T(8,128)S(1)} %get-tuple-element.89), channel_id=1, source_target_pairs={{0,4},{2,6},{4,0},{6,2},{8,12},{10,14},{12,8},{14,10},{1,5},{3,7},... | collective-permute-start | bytes 393224 | tf_op jit(solution)/shard_map/ppermute | solution.py:379
  160.3 19.3 %collective-permute-start.13 = (f32[256,128]{1,0:T(8,128)S(1)}, f32[256,128]{1,0:T(8,128)S(1)}, u32[]{:S(2)}, u32[]{:S(2)}) collective-permute-start(f32[256,128]{1,0:T(8,128)S(1)} %get-tuple-element.88), channel_id=1, source_target_pairs={{0,8},{2,10},{4,12},{6,14},{8,0},{10,2},{12,4},{14,6},{1,9},{3,11}... | collective-permute-start | bytes 393224 | tf_op jit(solution)/shard_map/ppermute | solution.py:379
  165.5 14.2 %collective-permute-start.14 = (f32[256,128]{1,0:T(8,128)S(1)}, f32[256,128]{1,0:T(8,128)S(1)}, u32[]{:S(2)}, u32[]{:S(2)}) collective-permute-start(f32[256,128]{1,0:T(8,128)S(1)} %get-tuple-element.87), channel_id=1, source_target_pairs={{0,12},{2,14},{4,8},{6,10},{8,4},{10,6},{12,0},{14,2},{1,13},{3,15... | collective-permute-start | bytes 393224 | tf_op jit(solution)/shard_map/ppermute | solution.py:379
